TPU v7x, 512 devices: a whole 4x4x16 slice. The times are simulated.
512 devices in a mesh: replica: 16 (over x_hi, y, core), tensor: 32 (over z, x_lo).
Axes of the slice: x: 4 (x_hi: 2, x_lo: 2; x = x_hi * 2 + x_lo), y: 4, z: 16, core: 2. Of those that a mesh axis runs over, the one named last changes fastest.
Arguments:
- step: int32 [1], replicated, may hold values from 0 to 999
- head_outputs: bfloat16 [16, 1536, 4096], P('replica', None, 'tensor'), may hold values from -70 to 70
- out_weight: bfloat16 [16, 4096, 5120], P('replica', 'tensor'), may hold values from -6 to 6
- cotangent: bfloat16 [16, 1536, 5120], P('replica', 'tensor'), may hold values from -40 to 40
Outputs:
- new_weight: bfloat16 [16, 4096, 5120], P('replica', 'tensor')
- head_grads: bfloat16 [16, 1536, 4096], P('replica', None, 'tensor')
All inputs are finite; a program needn't handle non-finite values.
Results may differ from a plain program's by a relative error of at most 0.0052.
Values may be sent and summed in bfloat16 or wider, within the bound.
No kernel may reach another device: no remote copies, remote signals or barrier semaphores. Data moves between devices by JAX's collectives and lax.ppermute only.
A program may use at most 64 MiB of HBM per device.

v0:
```python
from functools import partial

import jax
import jax.numpy as jnp
from jax import lax
from jax.sharding import PartitionSpec as P

step_rate = 0.5


def as_sent(shard):
    return jax.tree.map(lambda a: a.astype(jnp.bfloat16) if a.dtype == jnp.float32 else a, shard)


def swapped(block, axis, apart):
    count = lax.axis_size(axis)
    route = []
    for low in range(count):
        high = low | 1 << apart
        if high != low and high < count:
            route += [(low, high), (high, low)]
    return lax.ppermute(block, axis, route)


def trade(stepped, bit_number):
    return jax.tree.map(
        lambda part, own: part.astype(own.dtype),
        swapped(as_sent(stepped), "replica", bit_number),
        stepped,
    )


def per_device(step, head_outputs, out_weight, cotangent):
    local_heads = head_outputs[0]
    weight_rows = out_weight[0]
    grad_rows_local = cotangent[0]
    features = weight_rows.shape[0] * lax.axis_size("tensor")
    width = weight_rows.shape[1]
    multiplier = float(features) ** (-0.5)
    rows_in = lax.all_gather(grad_rows_local, "tensor", axis=0, tiled=True)
    grad_total = lax.dot_general(
        local_heads, rows_in, (((0,), (0,)), ((), ())), preferred_element_type=jnp.float32
    )
    input_total = multiplier * lax.dot_general(
        rows_in, weight_rows, (((1,), (1,)), ((), ())), preferred_element_type=jnp.float32
    )
    head_grads = input_total.astype(jnp.bfloat16)
    gradient = multiplier * grad_total
    squares = lax.psum(jnp.sum(gradient * gradient), "tensor")
    factor = jnp.minimum(1.0, jnp.sqrt(jnp.float32(features * width)) / jnp.sqrt(squares))
    stepped = (weight_rows.astype(jnp.float32) - step_rate * factor * gradient).astype(jnp.bfloat16)
    levels = min(3, lax.axis_size("replica") // 4 + 1)
    branches = [partial(trade, bit_number=number) for number in range(levels)]
    others = lax.switch(step[0] % levels, branches, stepped)
    new_weight = ((stepped.astype(jnp.float32) + others.astype(jnp.float32)) * 0.5).astype(
        jnp.bfloat16
    )
    return (new_weight[None], head_grads[None])


def solution(mesh):
    placed = (
        P(),
        P("replica", None, "tensor"),
        P("replica", "tensor", None),
        P("replica", "tensor", None),
    )
    return jax.shard_map(
        per_device,
        mesh=mesh,
        in_specs=placed,
        out_specs=(P("replica", "tensor", None), P("replica", None, "tensor")),
        check_vma=False,
    )
```

profile of v0, /device:TPU:4, one launch (start us, length us, event | category | flops | bytes accessed | tf_op | source)
XLA Modules:
  0.0 474.5 jit_solution(10879629287152725371)
XLA Ops:
  7.2 0.0 copy-start
  7.2 0.0 all-gather.3.cloned.1.call-start
  7.2 0.7 all-gather.3.cloned.1.call-update
  8.6 352.3 %all-gather.3.cloned.1.call-done = bf16[1,1536,5120]{2,1,0:T(8,128)(2,1)} async-done(((bf16[1,48,5120]{2,1,0:T(8,128)(2,1)}), bf16[1,1536,5120]{2,1,0:T(8,128)(2,1)}) %all-gather.3.cloned.1.call-update) | async-done | bytes 15728656 | tf_op jit(solution)/shard_map/all_gather | solution.py:40
  360.9 0.0 copy-done
  360.9 8.7 %multiply_reduce_fusion = (f32[]{:T(128)}, f32[128,5120]{1,0:T(8,128)S(1)}) fusion(bf16[1,1536,5120]{2,1,0:T(8,128)(2,1)} %all-gather.3.cloned.1.call-done, bf16[1,1536,128]{2,1,0:T(8,128)(2,1)S(1)} %copy-done), kind=kOutput, calls=%fused_computation.6 | convolution fusion | flops 2015232000 | bytes 18743300 | tf_op jit(solution)/shard_map/dot_general | solution.py:41
  369.6 63.3 %psum.7 = f32[]{:T(128)} all-reduce(f32[]{:T(128)} %get-tuple-element.15), channel_id=1, replica_groups=mesh['replica'=16,'tensor'=32] {'tensor'}, use_global_device_ids=true, to_apply=%region_1.0 | all-reduce | flops 1 | bytes 8 | tf_op jit(solution)/shard_map/psum | solution.py:49
  433.6 1.6 subtract_convert_fusion
  435.2 0.0 copy-start.1
  435.2 1.0 copy-done.1
  436.3 0.0 copy-start.2
  436.3 19.7 %conditional.4 = (bf16[128,5120]{1,0:T(8,128)(2,1)}) conditional(s32[]{:T(128)} %clamp.3, bf16[128,5120]{1,0:T(8,128)(2,1)S(1)} %subtract_convert_fusion, bf16[128,5120]{1,0:T(8,128)(2,1)S(1)} %subtract_convert_fusion, bf16[128,5120]{1,0:T(8,128)(2,1)S(1)} %subtract_convert_fusion), branch_computations={%region_2.3_spmd, %region_3.4_spmd, %region_4.5_spmd} | conditional | bytes 5242928
  436.3 3.5 collective-permute-start.1
  439.8 16.3 %collective-permute-done.1 = bf16[128,5120]{1,0:T(8,128)(2,1)} collective-permute-done((bf16[128,5120]{1,0:T(8,128)(2,1)S(1)}, bf16[128,5120]{1,0:T(8,128)(2,1)}, u32[]{:S(2)}, u32[]{:S(2)}) %collective-permute-start.1) | collective-permute-done | bytes 1310752 | tf_op jit(solution)/shard_map/cond/branch_1_fun/ppermute | solution.py:22
  456.0 3.2 fusion.13
  459.2 0.0 copy-done.2
  459.2 8.5 %fusion.10 = bf16[1,1536,128]{2,1,0:T(8,128)(2,1)} fusion(bf16[1,1536,5120]{2,1,0:T(8,128)(2,1)} %all-gather.3.cloned.1.call-done, bf16[1,128,5120]{2,1,0:T(8,128)(2,1)S(1)} %copy-done.2), kind=kOutput, calls=%fused_computation.9 | convolution fusion | flops 2013659136 | bytes 17432576 | tf_op jit(solution)/shard_map/dot_general | solution.py:44
Async XLA Ops:
  7.2 353.7 %copy-start = (bf16[1,1536,128]{2,1,0:T(8,128)(2,1)S(1)}, bf16[1,1536,128]{2,1,0:T(8,128)(2,1)}, u32[]{:S(2)}) copy-start(bf16[1,1536,128]{2,1,0:T(8,128)(2,1)} %param.8) | copy-start | bytes 1179652
  7.2 353.7 %all-gather.3.cloned.1.call-start = ((), (), s32[]{:S(2)}) async-start(), calls=%async_computation | async-start | bytes 16220160 | tf_op jit(solution)/shard_map/all_gather | solution.py:40
  435.2 1.1 copy-start.1
  436.3 22.9 %copy-start.2 = (bf16[1,128,5120]{2,1,0:T(8,128)(2,1)S(1)}, bf16[1,128,5120]{2,1,0:T(8,128)(2,1)}, u32[]{:S(2)}) copy-start(bf16[1,128,5120]{2,1,0:T(8,128)(2,1)} %param.9) | copy-start | bytes 3932164
  436.3 19.7 %collective-permute-start.1 = (bf16[128,5120]{1,0:T(8,128)(2,1)S(1)}, bf16[128,5120]{1,0:T(8,128)(2,1)}, u32[]{:S(2)}, u32[]{:S(2)}) collective-permute-start(bf16[128,5120]{1,0:T(8,128)(2,1)S(1)} %param.1), channel_id=1, source_target_pairs={{0,64},{64,0},{32,96},{96,32},{128,192},{192,128},{160,224},{224,1... | collective-permute-start | bytes 3932168 | tf_op jit(solution)/shard_map/cond/branch_1_fun/ppermute | solution.py:22
Sparse Core Ops, SparseCore 0:
  10.1 350.7 all-gather.2
where the time goes:
time: 476 us; the launch traced here: 474 us
  waiting for transfers between devices  369 us (78%)
  blocking collectives  63.3 us (13%)
  matrix products  17.2 us (4%)
  between operations  15.4 us (3%)
  other arithmetic  4.78 us (1%)
    all_gather x1, waiting for transfers between devices, per_device(): rows_in = lax.all_gather(grad_rows_local, 'tensor', axis=0, tiled=True)  352 us
    psum x1, blocking collectives, per_device(): squares = lax.psum(jnp.sum(gradient * gradient), 'tensor')  63.3 us
    ppermute x1, waiting for transfers between devices, swapped(): return lax.ppermute(block, axis, route)  16.3 us
  transfers between devices with their start and end apart: 2, of which 2 were waited for; matrix products, arithmetic and copies ran while one was open for 0% of the time, Pallas kernels for 0%

commit v1 on v0

v1 whole, which is shorter than its diff:
```python
from functools import partial

import jax
import jax.numpy as jnp
from jax import lax
from jax.sharding import Mesh, PartitionSpec as P

step_rate = 0.5
LEVELS = 3
PAIR = [(0, 1), (1, 0)]
Z = ("zh", "zl")


def to_partner(block, level):
    if level == 0:
        return lax.ppermute(block, "core", PAIR)
    return lax.ppermute(block, "y", [(i, i ^ level) for i in range(4)])


def one_step(level, head_outputs, out_weight, cotangent):
    heads = head_outputs[0]
    weight = out_weight[0]
    tokens = cotangent[0]
    rows, width = weight.shape
    half = width // 2
    features = rows * 32
    multiplier = float(features) ** (-0.5)
    x = lax.axis_index("x")

    def mine(block):
        return lax.dynamic_slice_in_dim(block, x * half, half, axis=1)

    def other(block):
        return lax.dynamic_slice_in_dim(block, (1 - x) * half, half, axis=1)

    def swap(block):
        return lax.ppermute(block, "x", PAIR)

    kept = mine(tokens)
    got = swap(other(tokens))
    pair_tokens = jnp.where(
        x == 0, jnp.concatenate([kept, got], 0), jnp.concatenate([got, kept], 0)
    )
    gathered = lax.all_gather(pair_tokens, Z, axis=0, tiled=True)

    heads_pair = jnp.concatenate([heads, swap(heads)], 1)
    weight_pair = jnp.concatenate([mine(weight), swap(other(weight))], 0)
    partner_weight = to_partner(weight, level)

    grad = multiplier * lax.dot_general(
        heads_pair, gathered, (((0,), (0,)), ((), ())), preferred_element_type=jnp.float32
    )
    squares = jnp.sum(grad * grad)
    grad16 = grad.astype(jnp.bfloat16)
    grad_here = grad16[:rows]
    grad_there = swap(grad16[rows:])
    partner_here = to_partner(grad_here, level)
    partner_there = to_partner(grad_there, level)

    squares = lax.psum(squares, "zl")
    squares = lax.psum(squares, "zh")
    squares = lax.psum(squares, "x")
    partner_squares = to_partner(squares, level)

    partial_heads = lax.dot_general(
        gathered, weight_pair, (((1,), (1,)), ((), ())), preferred_element_type=jnp.float32
    )
    from_pair = swap(partial_heads[:, rows:].astype(jnp.bfloat16))
    head_grads = (
        multiplier * (partial_heads[:, :rows] + from_pair.astype(jnp.float32))
    ).astype(jnp.bfloat16)

    def factor_of(total):
        return jnp.minimum(1.0, jnp.sqrt(jnp.float32(features * width)) / jnp.sqrt(total))

    def stepped(block, factor, gradient):
        new = block.astype(jnp.float32) - step_rate * factor * gradient.astype(jnp.float32)
        return new.astype(jnp.bfloat16).astype(jnp.float32)

    factor, partner_factor = factor_of(squares), factor_of(partner_squares)

    def both(here, there):
        return jnp.where(
            x == 0, jnp.concatenate([here, there], 1), jnp.concatenate([there, here], 1)
        )

    new_weight = (
        (
            stepped(weight, factor, both(grad_here, grad_there))
            + stepped(partner_weight, partner_factor, both(partner_here, partner_there))
        )
        * 0.5
    ).astype(jnp.bfloat16)
    return (new_weight[None], head_grads[None])


def per_device(step, head_outputs, out_weight, cotangent):
    branches = [partial(one_step, level) for level in range(LEVELS)]
    return lax.switch(step[0] % LEVELS, branches, head_outputs, out_weight, cotangent)


def solution(mesh):
    mesh = Mesh(
        mesh.devices.reshape(2, 4, 2, 4, 4, 2), ("x_hi", "y", "core", "zh", "zl", "x")
    )
    replica = ("x_hi", "y", "core")
    tensor = ("zh", "zl", "x")
    return jax.shard_map(
        per_device,
        mesh=mesh,
        in_specs=(
            P(),
            P(replica, None, tensor),
            P(replica, tensor, None),
            P(replica, tensor, None),
        ),
        out_specs=(P(replica, tensor, None), P(replica, None, tensor)),
        check_vma=False,
    )
```

time: 476 us -> 206 us (0.43)
  the two profiles are of different devices: /device:TPU:4 before, /device:TPU:1 now
where the time goes in v1:
time: 206 us; the launch traced here: 205 us
  waiting for transfers between devices  99.5 us (48%)
  starting transfers between devices  40.6 us (20%)
  blocking collectives  28.2 us (14%)
  between operations  14.7 us (7%)
  matrix products  9.89 us (5%)
  other arithmetic  7.33 us (4%)
  local copies, waits for them, and re-layouts  3.35 us (2%)
    all_gather x1, waiting for transfers between devices, one_step(): gathered = lax.all_gather(pair_tokens, Z, axis=0, tiled=True)  90.6 us
    ppermute x4, starting transfers between devices, to_partner(): return lax.ppermute(block, 'core', PAIR)  26 us
    psum x1, blocking collectives, one_step(): squares = lax.psum(squares, 'zh')  14.8 us
    ppermute x5, starting transfers between devices, swap(): return lax.ppermute(block, 'x', PAIR)  14.6 us
    psum x1, blocking collectives, one_step(): squares = lax.psum(squares, 'zl')  9.07 us
    ppermute x5, waiting for transfers between devices, swap(): return lax.ppermute(block, 'x', PAIR)  8.47 us
    dot_general x1, matrix products, one_step(): lax.dot_general(heads_pair, gathered, (((0,), (0,)), ((), ())), preferred...  6.56 us
    broadcast_in_dim x2, other arithmetic, one_step(): return (new_weight[None], head_grads[None])  6.4 us
  transfers between devices with their start and end apart: 10, of which 4 were waited for; matrix products, arithmetic and copies ran while one was open for 7% of the time, Pallas kernels for 0%

profile of v1, /device:TPU:1, one launch (start us, length us, event | category | flops | bytes accessed | tf_op | source)
XLA Modules:
  0.0 205.1 jit_solution(395638934290125419)
XLA Ops:
  7.8 190.4 %conditional.1 = (bf16[1,128,5120]{2,1,0:T(8,128)(2,1)}, bf16[1,1536,128]{2,1,0:T(8,128)(2,1)}) conditional(s32[]{:T(128)} %clamp.3, (bf16[1,128,5120]{2,1,0:T(8,128)(2,1)}, bf16[1,1536,128]{2,1,0:T(8,128)(2,1)}, bf16[1,48,5120]{2,1,0:T(8,128)(2,1)}) %tuple.19, (bf16[1,128,5120]{2,1,0:T(8,128)(2,1)}, ...), branch_computations={%region_0.5_spmd, %region_5.10_spmd, %region_10.15_spmd} | conditional | flops 4057972736 | bytes 128942920 | solution.py:99
  7.8 0.0 copy-start
  7.8 0.0 copy-start.12
  7.9 0.0 all-gather.4.cloned.1.call-start
  7.9 1.2 dynamic-slice_bitcast_fusion.3
  9.1 3.9 %collective-permute-start.1 = (bf16[48,2560]{1,0:T(8,128)(2,1)S(1)}, bf16[48,2560]{1,0:T(8,128)(2,1)S(1)}, u32[]{:S(2)}, u32[]{:S(2)}) collective-permute-start(bf16[48,2560]{1,0:T(8,128)(2,1)S(1)} %get-tuple-element.38), channel_id=1, source_target_pairs={{0,1},{1,0},{2,3},{3,2},{4,5},{5,4},{6,7},{7,6},{8,9},{9,8},{10,11... | collective-permute-start | bytes 737288 | tf_op jit(solution)/shard_map/cond/branch_0_fun/ppermute | solution.py:37
  13.1 3.6 %collective-permute-done.1 = bf16[48,2560]{1,0:T(8,128)(2,1)S(1)} collective-permute-done((bf16[48,2560]{1,0:T(8,128)(2,1)S(1)}, bf16[48,2560]{1,0:T(8,128)(2,1)S(1)}, u32[]{:S(2)}, u32[]{:S(2)}) %collective-permute-start.1) | collective-permute-done | bytes 245792 | tf_op jit(solution)/shard_map/cond/branch_0_fun/ppermute | solution.py:37
  16.7 0.9 maximum_select_fusion.2
  17.6 0.0 all-gather.4.cloned.1.call-update
  17.6 3.4 %collective-permute-start = (bf16[1536,128]{1,0:T(8,128)(2,1)}, bf16[1536,128]{1,0:T(8,128)(2,1)S(1)}, u32[]{:S(2)}, u32[]{:S(2)}) collective-permute-start(bf16[1536,128]{1,0:T(8,128)(2,1)} %bitcast.55), channel_id=1, source_target_pairs={{0,1},{1,0},{2,3},{3,2},{4,5},{5,4},{6,7},{7,6},{8,9},{9,8},{10,11... | collective-permute-start | bytes 1179656 | tf_op jit(solution)/shard_map/cond/branch_0_fun/ppermute | solution.py:37
  21.0 1.1 dynamic-slice_bitcast_fusion.1
  22.1 1.9 collective-permute-start.7
  24.1 11.1 %collective-permute-start.3 = (bf16[128,5120]{1,0:T(8,128)(2,1)S(1)}, bf16[128,5120]{1,0:T(8,128)(2,1)S(1)}, u32[]{:S(2)}, u32[]{:S(2)}) collective-permute-start(bf16[128,5120]{1,0:T(8,128)(2,1)S(1)} %bitcast.52), channel_id=1, source_target_pairs={{0,32},{32,0},{1,33},{33,1},{2,34},{34,2},{3,35},{35,3},{4,36},{36... | collective-permute-start | bytes 3932168 | tf_op jit(solution)/shard_map/cond/branch_0_fun/ppermute | solution.py:16
  35.2 0.0 collective-permute-done
  35.2 90.6 %all-gather.4.cloned.1.call-done = bf16[1536,2560]{1,0:T(8,128)(2,1)} async-done(((bf16[96,2560]{1,0:T(8,128)(2,1)}), bf16[1536,2560]{1,0:T(8,128)(2,1)}) %all-gather.4.cloned.1.call-update) | async-done | bytes 7864336 | tf_op jit(solution)/shard_map/cond/branch_0_fun/all_gather | solution.py:44
  125.8 6.6 %multiply_reduce_fusion = (f32[]{:T(128)}, bf16[256,2560]{1,0:T(8,128)(2,1)S(1)}) fusion(bf16[1536,2560]{1,0:T(8,128)(2,1)} %all-gather.4.cloned.1.call-done, bf16[1536,128]{1,0:T(8,128)(2,1)S(1)} %collective-permute-done, bf16[1536,128]{1,0:T(8,128)(2,1)S(1)} %bitcast.56), kind=kOutput, calls=%fused_computation.4 | convolution fusion | flops 2017460224 | bytes 9961476 | tf_op jit(solution)/shard_map/cond/branch_0_fun/dot_general | solution.py:50
  132.4 0.1 fusion.39
  132.5 3.2 %collective-permute-start.2 = (bf16[128,2560]{1,0:T(8,128)(2,1)S(1)}, bf16[128,2560]{1,0:T(8,128)(2,1)}, u32[]{:S(2)}, u32[]{:S(2)}) collective-permute-start(bf16[128,2560]{1,0:T(8,128)(2,1)S(1)} %get-tuple-element.36), channel_id=1, source_target_pairs={{0,1},{1,0},{2,3},{3,2},{4,5},{5,4},{6,7},{7,6},{8,9},{9,8},{10,11... | collective-permute-start | bytes 1966088 | tf_op jit(solution)/shard_map/cond/branch_0_fun/ppermute | solution.py:37
  135.7 0.0 collective-permute-done.7
  135.7 3.3 %fusion.1 = f32[1536,256]{1,0:T(8,128)S(1)} fusion(bf16[1536,2560]{1,0:T(8,128)(2,1)S(1)} %copy-done.9, bf16[128,2560]{1,0:T(8,128)(2,1)} %collective-permute-done.7, bf16[128,2560]{1,0:T(8,128)(2,1)S(1)} %copy-done.6), kind=kOutput, calls=%fused_computation.8 | convolution fusion | flops 2015887360 | bytes 10747904 | tf_op jit(solution)/shard_map/cond/branch_0_fun/dot_general | solution.py:65
  139.1 0.9 slice.75
  140.0 2.2 %collective-permute-start.8 = (bf16[1536,128]{1,0:T(8,128)(2,1)}, bf16[1536,128]{1,0:T(8,128)(2,1)}, u32[]{:S(2)}, u32[]{:S(2)}) collective-permute-start(bf16[1536,128]{1,0:T(8,128)(2,1)} %slice.75), channel_id=1, source_target_pairs={{0,1},{1,0},{2,3},{3,2},{4,5},{5,4},{6,7},{7,6},{8,9},{9,8},{10,11... | collective-permute-start | bytes 1179656 | tf_op jit(solution)/shard_map/cond/branch_0_fun/ppermute | solution.py:37
  142.1 3.1 %collective-permute-start.5 = (bf16[128,2560]{1,0:T(8,128)(2,1)S(1)}, bf16[128,2560]{1,0:T(8,128)(2,1)}, u32[]{:S(2)}, u32[]{:S(2)}) collective-permute-start(bf16[128,2560]{1,0:T(8,128)(2,1)S(1)} %get-tuple-element.35), channel_id=1, source_target_pairs={{0,32},{32,0},{1,33},{33,1},{2,34},{34,2},{3,35},{35,3},{4,36},{36... | collective-permute-start | bytes 1966088 | tf_op jit(solution)/shard_map/cond/branch_0_fun/ppermute | solution.py:16
  145.3 4.9 %collective-permute-done.2 = bf16[128,2560]{1,0:T(8,128)(2,1)} collective-permute-done((bf16[128,2560]{1,0:T(8,128)(2,1)S(1)}, bf16[128,2560]{1,0:T(8,128)(2,1)}, u32[]{:S(2)}, u32[]{:S(2)}) %collective-permute-start.2) | collective-permute-done | bytes 655392 | tf_op jit(solution)/shard_map/cond/branch_0_fun/ppermute | solution.py:37
  150.2 4.6 %collective-permute-start.6 = (bf16[128,2560]{1,0:T(8,128)(2,1)}, bf16[128,2560]{1,0:T(8,128)(2,1)}, u32[]{:S(2)}, u32[]{:S(2)}) collective-permute-start(bf16[128,2560]{1,0:T(8,128)(2,1)} %collective-permute-done.2), channel_id=1, source_target_pairs={{0,32},{32,0},{1,33},{33,1},{2,34},{34,2},{3,35},{35,3},{4,36},{36... | collective-permute-start | bytes 1966088 | tf_op jit(solution)/shard_map/cond/branch_0_fun/ppermute | solution.py:16
  154.8 9.1 %psum.54 = f32[]{:T(128)} all-reduce(f32[]{:T(128)} %get-tuple-element.31), channel_id=1, replica_groups=mesh['x_hi'=2,'y'=4,'core'=2,'zh'=4,'zl'=4,'x'=2] {'zl'}, use_global_device_ids=true, to_apply=%region_2.2 | all-reduce | flops 1 | bytes 8 | tf_op jit(solution)/shard_map/cond/branch_0_fun/psum | solution.py:60
  163.9 14.8 %psum.55 = f32[]{:T(128)} all-reduce(f32[]{:T(128)} %psum.54), channel_id=1, replica_groups=mesh['x_hi'=2,'y'=4,'core'=2,'zh'=4,'zl'=4,'x'=2] {'zh'}, use_global_device_ids=true, to_apply=%region_3.3 | all-reduce | flops 1 | bytes 8 | tf_op jit(solution)/shard_map/cond/branch_0_fun/psum | solution.py:61
  178.6 4.4 %psum.56 = f32[]{:T(128)} all-reduce(f32[]{:T(128)} %psum.55), channel_id=1, replica_groups=mesh['x_hi'=2,'y'=4,'core'=2,'zh'=4,'zl'=4,'x'=2] {'x'}, use_global_device_ids=true, to_apply=%region_4.4 | all-reduce | flops 1 | bytes 8 | tf_op jit(solution)/shard_map/cond/branch_0_fun/psum | solution.py:62
  183.0 7.1 %collective-permute-start.4 = (f32[]{:T(128)}, f32[]{:T(128)}, u32[]{:S(2)}, u32[]{:S(2)}) collective-permute-start(f32[]{:T(128)} %psum.56), channel_id=1, source_target_pairs={{0,32},{32,0},{1,33},{33,1},{2,34},{34,2},{3,35},{35,3},{4,36},{36... | collective-permute-start | bytes 20 | tf_op jit(solution)/shard_map/cond/branch_0_fun/ppermute | solution.py:16
  190.8 0.4 collective-permute-done.4
  191.8 2.1 %fusion.10 = bf16[1,1536,128]{2,1,0:T(8,128)(2,1)} fusion(bf16[1536,128]{1,0:T(8,128)(2,1)} %collective-permute-done.8, f32[1536,256]{1,0:T(8,128)} %copy-done.3), kind=kLoop, calls=%fused_computation.22 | loop fusion | flops 786432 | bytes 1572864 | tf_op jit(solution)/shard_map/cond/branch_0_fun/broadcast_in_dim | solution.py:94
  193.9 4.3 %fusion = bf16[1,128,5120]{2,1,0:T(8,128)(2,1)} fusion(bf16[128,5120]{1,0:T(8,128)(2,1)S(1)} %collective-permute-done.3, bf16[128,2560]{1,0:T(8,128)(2,1)} %collective-permute-done.2, bf16[128,2560]{1,0:T(8,128)(2,1)S(1)} %get-tuple-element.35, bf16[128,2560]{1,0:T(8,128)(2,1)} %collective-permute-done.6, bf16[128,2560]{1,0:T(8,128)(2,1)} %collective-permute-done.5, ...), kind=kLoop, calls=%fused_computation.5 | loop fusion | flops 21626880 | bytes 6553609 | tf_op jit(solution)/shard_map/cond/branch_0_fun/broadcast_in_dim | solution.py:94
  (12 shorter events, 0.0 us)
Async XLA Ops:
  7.8 13.1 %copy-start = (bf16[1,128,5120]{2,1,0:T(8,128)(2,1)S(1)}, bf16[1,128,5120]{2,1,0:T(8,128)(2,1)}, u32[]{:S(2)}) copy-start(bf16[1,128,5120]{2,1,0:T(8,128)(2,1)} %get-tuple-element.18) | copy-start | bytes 3932164 | tf_op jit(solution)/shard_map/cond
  7.8 118.0 %copy-start.12 = (bf16[1,1536,128]{2,1,0:T(8,128)(2,1)S(1)}, bf16[1,1536,128]{2,1,0:T(8,128)(2,1)}, u32[]{:S(2)}) copy-start(bf16[1,1536,128]{2,1,0:T(8,128)(2,1)} %get-tuple-element.19) | copy-start | bytes 1179652 | tf_op jit(solution)/shard_map/cond
  7.9 117.9 %all-gather.4.cloned.1.call-start = ((), (), s32[]{:S(2)}) async-start(), calls=%async_computation | async-start | bytes 8355840 | tf_op jit(solution)/shard_map/cond/branch_0_fun/all_gather | solution.py:44
  9.1 7.5 %collective-permute-start.1 = (bf16[48,2560]{1,0:T(8,128)(2,1)S(1)}, bf16[48,2560]{1,0:T(8,128)(2,1)S(1)}, u32[]{:S(2)}, u32[]{:S(2)}) collective-permute-start(bf16[48,2560]{1,0:T(8,128)(2,1)S(1)} %get-tuple-element.38), channel_id=1, source_target_pairs={{0,1},{1,0},{2,3},{3,2},{4,5},{5,4},{6,7},{7,6},{8,9},{9,8},{10,11... | collective-permute-start | bytes 737288 | tf_op jit(solution)/shard_map/cond/branch_0_fun/ppermute | solution.py:37
  17.6 17.6 %collective-permute-start = (bf16[1536,128]{1,0:T(8,128)(2,1)}, bf16[1536,128]{1,0:T(8,128)(2,1)S(1)}, u32[]{:S(2)}, u32[]{:S(2)}) collective-permute-start(bf16[1536,128]{1,0:T(8,128)(2,1)} %bitcast.55), channel_id=1, source_target_pairs={{0,1},{1,0},{2,3},{3,2},{4,5},{5,4},{6,7},{7,6},{8,9},{9,8},{10,11... | collective-permute-start | bytes 1179656 | tf_op jit(solution)/shard_map/cond/branch_0_fun/ppermute | solution.py:37
  22.1 113.6 %collective-permute-start.7 = (bf16[128,2560]{1,0:T(8,128)(2,1)}, bf16[128,2560]{1,0:T(8,128)(2,1)}, u32[]{:S(2)}, u32[]{:S(2)}) collective-permute-start(bf16[128,2560]{1,0:T(8,128)(2,1)} %get-tuple-element.34), channel_id=1, source_target_pairs={{0,1},{1,0},{2,3},{3,2},{4,5},{5,4},{6,7},{7,6},{8,9},{9,8},{10,11... | collective-permute-start | bytes 1966088 | tf_op jit(solution)/shard_map/cond/branch_0_fun/ppermute | solution.py:37
  24.1 169.8 %collective-permute-start.3 = (bf16[128,5120]{1,0:T(8,128)(2,1)S(1)}, bf16[128,5120]{1,0:T(8,128)(2,1)S(1)}, u32[]{:S(2)}, u32[]{:S(2)}) collective-permute-start(bf16[128,5120]{1,0:T(8,128)(2,1)S(1)} %bitcast.52), channel_id=1, source_target_pairs={{0,32},{32,0},{1,33},{33,1},{2,34},{34,2},{3,35},{35,3},{4,36},{36... | collective-permute-start | bytes 3932168 | tf_op jit(solution)/shard_map/cond/branch_0_fun/ppermute | solution.py:16
  125.8 9.9 %copy-start.9 = (bf16[1536,2560]{1,0:T(8,128)(2,1)S(1)}, bf16[1536,2560]{1,0:T(8,128)(2,1)}, u32[]{:S(2)}) copy-start(bf16[1536,2560]{1,0:T(8,128)(2,1)} %all-gather.4.cloned.1.call-done) | copy-start | bytes 23592964 | tf_op jit(solution)/shard_map/cond
  132.4 3.4 %copy-start.6 = (bf16[128,2560]{1,0:T(8,128)(2,1)S(1)}, bf16[128,2560]{1,0:T(8,128)(2,1)}, u32[]{:S(2)}) copy-start(bf16[128,2560]{1,0:T(8,128)(2,1)} %get-tuple-element.33) | copy-start | bytes 1966084 | tf_op jit(solution)/shard_map/cond
  132.5 17.7 %collective-permute-start.2 = (bf16[128,2560]{1,0:T(8,128)(2,1)S(1)}, bf16[128,2560]{1,0:T(8,128)(2,1)}, u32[]{:S(2)}, u32[]{:S(2)}) collective-permute-start(bf16[128,2560]{1,0:T(8,128)(2,1)S(1)} %get-tuple-element.36), channel_id=1, source_target_pairs={{0,1},{1,0},{2,3},{3,2},{4,5},{5,4},{6,7},{7,6},{8,9},{9,8},{10,11... | collective-permute-start | bytes 1966088 | tf_op jit(solution)/shard_map/cond/branch_0_fun/ppermute | solution.py:37
  139.1 3.1 %copy-start.3 = (f32[1536,256]{1,0:T(8,128)}, f32[1536,256]{1,0:T(8,128)S(1)}, u32[]{:S(2)}) copy-start(f32[1536,256]{1,0:T(8,128)S(1)} %fusion.1) | copy-start | bytes 4718596 | tf_op jit(solution)/shard_map/cond
  140.0 51.8 %collective-permute-start.8 = (bf16[1536,128]{1,0:T(8,128)(2,1)}, bf16[1536,128]{1,0:T(8,128)(2,1)}, u32[]{:S(2)}, u32[]{:S(2)}) collective-permute-start(bf16[1536,128]{1,0:T(8,128)(2,1)} %slice.75), channel_id=1, source_target_pairs={{0,1},{1,0},{2,3},{3,2},{4,5},{5,4},{6,7},{7,6},{8,9},{9,8},{10,11... | collective-permute-start | bytes 1179656 | tf_op jit(solution)/shard_map/cond/branch_0_fun/ppermute | solution.py:37
  142.1 51.8 %collective-permute-start.5 = (bf16[128,2560]{1,0:T(8,128)(2,1)S(1)}, bf16[128,2560]{1,0:T(8,128)(2,1)}, u32[]{:S(2)}, u32[]{:S(2)}) collective-permute-start(bf16[128,2560]{1,0:T(8,128)(2,1)S(1)} %get-tuple-element.35), channel_id=1, source_target_pairs={{0,32},{32,0},{1,33},{33,1},{2,34},{34,2},{3,35},{35,3},{4,36},{36... | collective-permute-start | bytes 1966088 | tf_op jit(solution)/shard_map/cond/branch_0_fun/ppermute | solution.py:16
  150.2 43.7 %collective-permute-start.6 = (bf16[128,2560]{1,0:T(8,128)(2,1)}, bf16[128,2560]{1,0:T(8,128)(2,1)}, u32[]{:S(2)}, u32[]{:S(2)}) collective-permute-start(bf16[128,2560]{1,0:T(8,128)(2,1)} %collective-permute-done.2), channel_id=1, source_target_pairs={{0,32},{32,0},{1,33},{33,1},{2,34},{34,2},{3,35},{35,3},{4,36},{36... | collective-permute-start | bytes 1966088 | tf_op jit(solution)/shard_map/cond/branch_0_fun/ppermute | solution.py:16
  183.0 8.2 %collective-permute-start.4 = (f32[]{:T(128)}, f32[]{:T(128)}, u32[]{:S(2)}, u32[]{:S(2)}) collective-permute-start(f32[]{:T(128)} %psum.56), channel_id=1, source_target_pairs={{0,32},{32,0},{1,33},{33,1},{2,34},{34,2},{3,35},{35,3},{4,36},{36... | collective-permute-start | bytes 20 | tf_op jit(solution)/shard_map/cond/branch_0_fun/ppermute | solution.py:16
Sparse Core Ops, SparseCore 0:
  17.7 108.0 all-gather.3

commit v2 on v1

v2 whole, which is shorter than its diff:
```python
from functools import partial

import jax
import jax.numpy as jnp
from jax import lax
from jax.experimental import pallas as pl
from jax.experimental.pallas import tpu as pltpu
from jax.sharding import Mesh, PartitionSpec as P

step_rate = 0.5
PAIR = [(0, 1), (1, 0)]
Z = ("zh", "zl")
PARTNER_AXES = ("core", "yl", "yh")
VMEM_BYTES = 48 * 1024 * 1024


def products_kernel(
    heads_ref, tokens_ref, weight_ref, here_ref, there_ref, squares_ref, part_here_ref,
    part_there_ref, total, sums,
):
    rows = here_ref.shape[0]
    step, last = pl.program_id(0), pl.num_programs(0) - 1
    block = tokens_ref[...]
    grad = jnp.dot(heads_ref[...], block, preferred_element_type=jnp.float32)
    here_ref[...] = grad[:rows].astype(here_ref.dtype)
    there_ref[...] = grad[rows:].astype(there_ref.dtype)
    part = lax.dot_general(
        block, weight_ref[...], (((1,), (1,)), ((), ())), preferred_element_type=jnp.float32
    )
    column_sums = jnp.sum(grad * grad, axis=0, keepdims=True)

    @pl.when(step == 0)
    def _():
        total[...] = part
        sums[...] = column_sums

    @pl.when(step > 0)
    def _():
        total[...] += part
        sums[...] += column_sums

    @pl.when(step == last)
    def _():
        part_here_ref[...] = total[:, :rows]
        part_there_ref[...] = total[:, rows:].astype(part_there_ref.dtype)
        squares_ref[0, 0] = jnp.sum(sums[...])


def products(heads_t, tokens, weight, blocks=5):
    pair_rows, count = heads_t.shape
    rows, width = pair_rows // 2, tokens.shape[1]
    cols = width // blocks
    return pl.pallas_call(
        products_kernel,
        grid=(blocks,),
        in_specs=[
            pl.BlockSpec((pair_rows, count), lambda i: (0, 0)),
            pl.BlockSpec((count, cols), lambda i: (0, i)),
            pl.BlockSpec((pair_rows, cols), lambda i: (0, i)),
        ],
        out_specs=[
            pl.BlockSpec((rows, cols), lambda i: (0, i)),
            pl.BlockSpec((rows, cols), lambda i: (0, i)),
            pl.BlockSpec((1, 1), lambda i: (0, 0), memory_space=pltpu.SMEM),
            pl.BlockSpec((count, rows), lambda i: (0, 0)),
            pl.BlockSpec((count, rows), lambda i: (0, 0)),
        ],
        out_shape=[
            jax.ShapeDtypeStruct((rows, width), jnp.bfloat16),
            jax.ShapeDtypeStruct((rows, width), jnp.bfloat16),
            jax.ShapeDtypeStruct((1, 1), jnp.float32),
            jax.ShapeDtypeStruct((count, rows), jnp.float32),
            jax.ShapeDtypeStruct((count, rows), jnp.bfloat16),
        ],
        scratch_shapes=[
            pltpu.VMEM((count, pair_rows), jnp.float32),
            pltpu.VMEM((1, cols), jnp.float32),
        ],
        compiler_params=pltpu.CompilerParams(vmem_limit_bytes=VMEM_BYTES),
        cost_estimate=pl.CostEstimate(
            flops=4 * pair_rows * count * width,
            bytes_accessed=2 * (count * width + 3 * pair_rows * width + 4 * count * rows),
            transcendentals=0,
        ),
        name="products",
    )(heads_t, tokens, weight)


def finish_kernel(
    multiplier, spot_ref, squares_ref, weight_ref, partner_ref, here_ref, there_ref,
    partner_here_ref, partner_there_ref, part_ref, from_pair_ref, new_ref, heads_ref,
):
    entries = jnp.float32(4096 * 5120)
    here = pl.program_id(0) == 0
    own = spot_ref[1]

    def scale(index):
        total = jnp.full((8, 128), squares_ref[index], jnp.float32) * (multiplier * multiplier)
        factor = jnp.minimum(1.0, jnp.sqrt(entries) / jnp.sqrt(total))
        return (step_rate * multiplier * factor)[:1, :1]

    def stepped(block_ref, amount, first_ref, second_ref):
        grad = jnp.where(here, first_ref[...], second_ref[...]).astype(jnp.float32)
        new = block_ref[...].astype(jnp.float32) - amount * grad
        return new.astype(jnp.bfloat16).astype(jnp.float32)

    mine = stepped(weight_ref, scale(own), here_ref, there_ref)
    theirs = stepped(partner_ref, scale(1 - own), partner_here_ref, partner_there_ref)
    new_ref[...] = ((mine + theirs) * 0.5).astype(new_ref.dtype)
    heads_ref[...] = (
        multiplier * (part_ref[...] + from_pair_ref[...].astype(jnp.float32))
    ).astype(heads_ref.dtype)


def finish(multiplier, spot, squares, weight, partner, grads, partner_grads, part, from_pair, blocks=2):
    rows, width = weight.shape
    half = width // 2
    cols = half // blocks
    count = part.shape[0]
    piece = count // (2 * blocks)

    def whole(h, i, spot_ref, squares_ref):
        return (0, jnp.where(h == 0, spot_ref[0], 1 - spot_ref[0]) * blocks + i)

    first = lambda h, i, *_: (0, jnp.where(h == 0, i, blocks - 1))
    second = lambda h, i, *_: (0, jnp.where(h == 0, 0, i))
    down = lambda h, i, *_: (h * blocks + i, 0)
    wide = pl.BlockSpec((rows, cols), whole)
    return pl.pallas_call(
        partial(finish_kernel, multiplier),
        grid_spec=pltpu.PrefetchScalarGridSpec(
            num_scalar_prefetch=2,
            grid=(2, blocks),
            in_specs=[
                wide,
                wide,
                pl.BlockSpec((rows, cols), first),
                pl.BlockSpec((rows, cols), second),
                pl.BlockSpec((rows, cols), first),
                pl.BlockSpec((rows, cols), second),
                pl.BlockSpec((piece, rows), down),
                pl.BlockSpec((piece, rows), down),
            ],
            out_specs=[wide, pl.BlockSpec((piece, rows), down)],
        ),
        out_shape=[
            jax.ShapeDtypeStruct((rows, width), jnp.bfloat16),
            jax.ShapeDtypeStruct((count, rows), jnp.bfloat16),
        ],
        compiler_params=pltpu.CompilerParams(vmem_limit_bytes=VMEM_BYTES),
        cost_estimate=pl.CostEstimate(
            flops=8 * rows * width, bytes_accessed=10 * rows * width + 8 * count * rows,
            transcendentals=0,
        ),
        name="finish",
    )(spot, squares, weight, partner, *grads, *partner_grads, part, from_pair)


def one_step(level, head_outputs, out_weight, cotangent):
    heads = head_outputs[0]
    weight = out_weight[0]
    tokens = cotangent[0]
    rows, width = weight.shape
    half = width // 2
    partner_axis = PARTNER_AXES[level]
    x = lax.axis_index("x")
    own = lax.axis_index(partner_axis)

    def mine(block):
        return lax.dynamic_slice_in_dim(block, x * half, half, axis=1)

    def other(block):
        return lax.dynamic_slice_in_dim(block, (1 - x) * half, half, axis=1)

    def swap(block):
        return lax.ppermute(block, "x", PAIR)

    def to_partner(block):
        return lax.ppermute(block, partner_axis, PAIR)

    kept = mine(tokens)
    got = swap(other(tokens))
    pair_tokens = jnp.where(
        x == 0, jnp.concatenate([kept, got], 0), jnp.concatenate([got, kept], 0)
    )
    gathered = lax.all_gather(pair_tokens, Z, axis=0, tiled=True)

    heads_t = jnp.concatenate([heads, swap(heads)], 1).T
    weight_pair = jnp.concatenate([mine(weight), swap(other(weight))], 0)
    partner_weight = to_partner(weight)

    gathered, partner_weight = lax.optimization_barrier((gathered, partner_weight))
    here, there, squares, part_here, part_there = products(heads_t, gathered, weight_pair)
    there = swap(there)
    partner_here = to_partner(here)
    squares = jnp.where(jnp.arange(2) == own, squares[0, 0], 0.0)
    squares = lax.psum(squares, "zl")
    squares, there = lax.optimization_barrier((squares, there))
    partner_there = to_partner(there)
    squares = lax.psum(squares, "zh")
    squares, part_there = lax.optimization_barrier((squares, part_there))
    from_pair = swap(part_there)
    squares = lax.psum(squares, (partner_axis, "x"))

    return (
        own, squares, partner_weight, (here, there), (partner_here, partner_there), part_here,
        from_pair,
    )


def per_device(step, head_outputs, out_weight, cotangent):
    branches = [partial(one_step, level) for level in range(len(PARTNER_AXES))]
    own, squares, partner_weight, grads, partner_grads, part_here, from_pair = lax.switch(
        step[0] % len(PARTNER_AXES), branches, head_outputs, out_weight, cotangent
    )
    weight = out_weight[0]
    new_weight, head_grads = finish(
        float(weight.shape[0] * 32) ** (-0.5),
        jnp.stack([lax.axis_index("x"), own]).astype(jnp.int32),
        squares,
        weight,
        partner_weight,
        grads,
        partner_grads,
        part_here,
        from_pair,
    )
    return (new_weight[None], head_grads[None])


def solution(mesh):
    mesh = Mesh(
        mesh.devices.reshape(2, 2, 2, 2, 4, 4, 2), ("x_hi", "yh", "yl", "core", "zh", "zl", "x")
    )
    replica = ("x_hi", "yh", "yl", "core")
    tensor = ("zh", "zl", "x")
    return jax.shard_map(
        per_device,
        mesh=mesh,
        in_specs=(
            P(),
            P(replica, None, tensor),
            P(replica, tensor, None),
            P(replica, tensor, None),
        ),
        out_specs=(P(replica, tensor, None), P(replica, None, tensor)),
        check_vma=False,
    )
```

time: 206 us -> 201 us (0.976)
  the two profiles are of different devices: /device:TPU:1 before, /device:TPU:4 now
where the time goes in v2:
time: 201 us; the launch traced here: 200 us
  waiting for transfers between devices  98.1 us (49%)
  blocking collectives  37.9 us (19%)
  starting transfers between devices  29.5 us (15%)
  Pallas kernels  14.7 us (7%)
  between operations  14.7 us (7%)
  other arithmetic  2.82 us (1%)
  local copies, waits for them, and re-layouts  2.32 us (1%)
    all_gather x1, waiting for transfers between devices, one_step(): gathered = lax.all_gather(pair_tokens, Z, axis=0, tiled=True)  72 us
    ppermute x5, waiting for transfers between devices, swap(): return lax.ppermute(block, 'x', PAIR)  25.9 us
    psum x1, blocking collectives, one_step(): squares = lax.psum(squares, 'zh')  15.4 us
    ppermute x5, starting transfers between devices, swap(): return lax.ppermute(block, 'x', PAIR)  15.2 us
    ppermute x3, starting transfers between devices, to_partner(): return lax.ppermute(block, partner_axis, PAIR)  14.3 us
    psum x1, blocking collectives, one_step(): squares = lax.psum(squares, (partner_axis, 'x'))  11.9 us
    psum x1, blocking collectives, one_step(): squares = lax.psum(squares, 'zl')  10.6 us
    pallas_call x1, Pallas kernels, products(): pl.pallas_call(products_kernel, grid=(blocks,), in_specs=[pl.BlockSpec((p...  8.92 us
  transfers between devices with their start and end apart: 9, of which 4 were waited for; matrix products, arithmetic and copies ran while one was open for 1% of the time, Pallas kernels for 0%

profile of v2, /device:TPU:4, one launch (start us, length us, event | category | flops | bytes accessed | tf_op | source)
XLA Modules:
  0.0 200.3 jit_solution(11560511306711982886)
XLA Ops:
  7.8 179.8 %conditional.2 = (u32[]{:T(128)}, f32[2]{0:T(128)S(1)}, bf16[128,5120]{1,0:T(8,128)(2,1)}, bf16[128,2560]{1,0:T(8,128)(2,1)}, bf16[128,2560]{1,0:T(8,128)(2,1)},...) conditional(s32[]{:T(128)} %clamp.3, ...), branch_computations={%region_0.4_spmd, %region_4.8_spmd, %region_8.12_spmd} | conditional | flops 4032937984 | bytes 79921944
  7.9 0.0 copy-start.2
  7.9 0.0 all-gather.8.cloned.1.call-start
  7.9 1.2 dynamic-slice_bitcast_fusion.11
  9.1 3.1 %collective-permute-start.17 = (bf16[48,2560]{1,0:T(8,128)(2,1)S(1)}, bf16[48,2560]{1,0:T(8,128)(2,1)S(1)}, u32[]{:S(2)}, u32[]{:S(2)}) collective-permute-start(bf16[48,2560]{1,0:T(8,128)(2,1)S(1)} %get-tuple-element.114), channel_id=1, source_target_pairs={{0,1},{1,0},{2,3},{3,2},{4,5},{5,4},{6,7},{7,6},{8,9},{9,8},{10,11... | collective-permute-start | bytes 737288 | tf_op jit(solution)/shard_map/cond/branch_2_fun/ppermute | solution.py:176
  12.2 6.5 %collective-permute-done.17 = bf16[48,2560]{1,0:T(8,128)(2,1)S(1)} collective-permute-done((bf16[48,2560]{1,0:T(8,128)(2,1)S(1)}, bf16[48,2560]{1,0:T(8,128)(2,1)S(1)}, u32[]{:S(2)}, u32[]{:S(2)}) %collective-permute-start.17) | collective-permute-done | bytes 245792 | tf_op jit(solution)/shard_map/cond/branch_2_fun/ppermute | solution.py:176
  18.7 0.9 maximum_select_fusion.2
  19.6 0.0 all-gather.8.cloned.1.call-update
  19.6 5.2 %collective-permute-start.18 = (bf16[128,5120]{1,0:T(8,128)(2,1)S(1)}, bf16[128,5120]{1,0:T(8,128)(2,1)}, u32[]{:S(2)}, u32[]{:S(2)}) collective-permute-start(bf16[128,5120]{1,0:T(8,128)(2,1)S(1)} %bitcast.48), channel_id=1, source_target_pairs={{0,128},{128,0},{1,129},{129,1},{2,130},{130,2},{3,131},{131,3},{4... | collective-permute-start | bytes 3932168 | tf_op jit(solution)/shard_map/cond/branch_2_fun/ppermute | solution.py:179
  24.9 0.9 dynamic-slice_bitcast_fusion.9
  25.8 3.1 %collective-permute-start.19 = (bf16[128,2560]{1,0:T(8,128)(2,1)S(1)}, bf16[128,2560]{1,0:T(8,128)(2,1)}, u32[]{:S(2)}, u32[]{:S(2)}) collective-permute-start(bf16[128,2560]{1,0:T(8,128)(2,1)S(1)} %get-tuple-element.112), channel_id=1, source_target_pairs={{0,1},{1,0},{2,3},{3,2},{4,5},{5,4},{6,7},{7,6},{8,9},{9,8},{10,11... | collective-permute-start | bytes 1966088 | tf_op jit(solution)/shard_map/cond/branch_2_fun/ppermute | solution.py:176
  28.9 0.2 copy.8
  29.1 0.0 copy-start.8
  29.1 2.9 %collective-permute-start.16 = (bf16[1536,128]{0,1:T(8,128)(2,1)S(1)}, bf16[1536,128]{0,1:T(8,128)(2,1)S(1)}, u32[]{:S(2)}, u32[]{:S(2)}) collective-permute-start(bf16[1536,128]{0,1:T(8,128)(2,1)S(1)} %bitcast.53), channel_id=1, source_target_pairs={{0,1},{1,0},{2,3},{3,2},{4,5},{5,4},{6,7},{7,6},{8,9},{9,8},{10,11... | collective-permute-start | bytes 1179656 | tf_op jit(solution)/shard_map/cond/branch_2_fun/ppermute | solution.py:176
  32.0 19.4 %collective-permute-done.16 = bf16[1536,128]{0,1:T(8,128)(2,1)S(1)} collective-permute-done((bf16[1536,128]{0,1:T(8,128)(2,1)S(1)}, bf16[1536,128]{0,1:T(8,128)(2,1)S(1)}, u32[]{:S(2)}, u32[]{:S(2)}) %collective-permute-start.16) | collective-permute-done | bytes 393248 | tf_op jit(solution)/shard_map/cond/branch_2_fun/ppermute | solution.py:176
  51.4 0.1 maximum_bitcast_fusion.2.heads_ref
  51.5 0.0 collective-permute-done.19
  51.5 1.2 pad_maximum_fusion.2.weight_ref
  52.7 0.2 collective-permute-done.18
  52.9 72.0 %all-gather.8.cloned.1.call-done.tokens_ref = bf16[1536,2560]{1,0:T(8,128)(2,1)} async-done(((bf16[96,2560]{1,0:T(8,128)(2,1)}), bf16[1536,2560]{1,0:T(8,128)(2,1)}) %all-gather.8.cloned.1.call-update) | async-done | bytes 7864336 | tf_op jit(solution)/shard_map/cond/branch_2_fun/all_gather | solution.py:186
  124.9 8.9 %products.5 = (bf16[128,2560]{1,0:T(8,128)(2,1)}, bf16[128,2560]{1,0:T(8,128)(2,1)S(1)}, f32[1,1]{1,0:T(1,128)}, f32[1536,128]{1,0:T(8,128)}, bf16[1536,128]{1,0:T(8,128)(2,1)S(1)}) custom-call(bf16[256,1536]{1,0:T(8,128)(2,1)S(1)} %maximum_bitcast_fusion.2.heads_ref, bf16[1536,2560]{1,0:T(8,128)(2,1)} %all-gather.8.cloned.1.call-done.tokens_ref, ...), custom_call_target="tpu_custom_call" | custom-call | flops 4026531840 | bytes 13369344 | tf_op jit(solution)/shard_map/cond/branch_2_fun/products/pallas_call | solution.py:53
  133.8 3.1 %collective-permute-start.20 = (bf16[128,2560]{1,0:T(8,128)(2,1)S(1)}, bf16[128,2560]{1,0:T(8,128)(2,1)}, u32[]{:S(2)}, u32[]{:S(2)}) collective-permute-start(bf16[128,2560]{1,0:T(8,128)(2,1)S(1)} %get-tuple-element.61), channel_id=1, source_target_pairs={{0,1},{1,0},{2,3},{3,2},{4,5},{5,4},{6,7},{7,6},{8,9},{9,8},{10,11... | collective-permute-start | bytes 1966088 | tf_op jit(solution)/shard_map/cond/branch_2_fun/ppermute | solution.py:176
  136.9 0.6 compare_select_fusion.2
  137.6 10.6 %psum.60 = f32[2]{0:T(128)S(1)} all-reduce(f32[2]{0:T(128)S(1)} %compare_select_fusion.2), channel_id=1, replica_groups=mesh['x_hi'=2,'yh'=2,'yl'=2,'core'=2,'zh'=4,'zl'=4,'x'=2] {'zl'}, use_global_device_ids=true, to_apply=%region_9.9 | all-reduce | flops 2 | bytes 16 | tf_op jit(solution)/shard_map/cond/branch_2_fun/psum | solution.py:197
  148.1 4.9 %collective-permute-start.21 = (bf16[128,2560]{1,0:T(8,128)(2,1)}, bf16[128,2560]{1,0:T(8,128)(2,1)}, u32[]{:S(2)}, u32[]{:S(2)}) collective-permute-start(bf16[128,2560]{1,0:T(8,128)(2,1)} %get-tuple-element.136), channel_id=1, source_target_pairs={{0,128},{128,0},{1,129},{129,1},{2,130},{130,2},{3,131},{131,3},{4... | collective-permute-start | bytes 1966088 | tf_op jit(solution)/shard_map/cond/branch_2_fun/ppermute | solution.py:179
  153.1 0.0 collective-permute-done.20
  153.1 4.1 %collective-permute-start.22 = (bf16[128,2560]{1,0:T(8,128)(2,1)}, bf16[128,2560]{1,0:T(8,128)(2,1)}, u32[]{:S(2)}, u32[]{:S(2)}) collective-permute-start(bf16[128,2560]{1,0:T(8,128)(2,1)} %collective-permute-done.20), channel_id=1, source_target_pairs={{0,128},{128,0},{1,129},{129,1},{2,130},{130,2},{3,131},{131,3},{4... | collective-permute-start | bytes 1966088 | tf_op jit(solution)/shard_map/cond/branch_2_fun/ppermute | solution.py:179
  157.2 15.4 %psum.61 = f32[2]{0:T(128)S(1)} all-reduce(f32[2]{0:T(128)S(1)} %psum.60), channel_id=1, replica_groups=mesh['x_hi'=2,'yh'=2,'yl'=2,'core'=2,'zh'=4,'zl'=4,'x'=2] {'zh'}, use_global_device_ids=true, to_apply=%region_10.10 | all-reduce | flops 2 | bytes 16 | tf_op jit(solution)/shard_map/cond/branch_2_fun/psum | solution.py:200
  172.6 3.1 %collective-permute-start.23 = (bf16[1536,128]{1,0:T(8,128)(2,1)S(1)}, bf16[1536,128]{1,0:T(8,128)(2,1)}, u32[]{:S(2)}, u32[]{:S(2)}) collective-permute-start(bf16[1536,128]{1,0:T(8,128)(2,1)S(1)} %get-tuple-element.69), channel_id=1, source_target_pairs={{0,1},{1,0},{2,3},{3,2},{4,5},{5,4},{6,7},{7,6},{8,9},{9,8},{10,11... | collective-permute-start | bytes 1179656 | tf_op jit(solution)/shard_map/cond/branch_2_fun/ppermute | solution.py:176
  175.7 11.9 %psum.62 = f32[2]{0:T(128)S(1)} all-reduce(f32[2]{0:T(128)S(1)} %psum.61), channel_id=1, replica_groups=mesh['x_hi'=2,'yh'=2,'yl'=2,'core'=2,'zh'=4,'zl'=4,'x'=2] {'yh','x'}, use_global_device_ids=true, to_apply=%region_11.11 | all-reduce | flops 2 | bytes 16 | tf_op jit(solution)/shard_map/cond/branch_2_fun/psum | solution.py:203
  187.6 0.1 pad_add_fusion.spot_ref
  187.7 5.7 %finish.1 = (bf16[128,5120]{1,0:T(8,128)(2,1)}, bf16[1536,128]{1,0:T(8,128)(2,1)}) custom-call(s32[2]{0:T(128)S(1)} %pad_add_fusion.spot_ref, f32[2]{0:T(128)S(1)} %get-tuple-element.84.squares_ref, bf16[128,5120]{1,0:T(8,128)(2,1)} %bitcast.45, bf16[128,5120]{1,0:T(8,128)(2,1)} %get-tuple-element.85.partner_ref, ...), custom_call_target="tpu_custom_call" | custom-call | flops 5242880 | bytes 8126464 | tf_op jit(solution)/shard_map/finish/pallas_call | solution.py:129
  (7 shorter events, 0.0 us)
Async XLA Ops:
  7.9 11.8 %copy-start.2 = (bf16[1,128,5120]{2,1,0:T(8,128)(2,1)S(1)}, bf16[1,128,5120]{2,1,0:T(8,128)(2,1)}, u32[]{:S(2)}) copy-start(bf16[1,128,5120]{2,1,0:T(8,128)(2,1)} %get-tuple-element.58) | copy-start | bytes 3932164 | tf_op jit(solution)/shard_map/conditional
  7.9 117.0 %all-gather.8.cloned.1.call-start = ((), (), s32[]{:S(2)}) async-start(), calls=%async_computation.2 | async-start | bytes 8355840 | tf_op jit(solution)/shard_map/cond/branch_2_fun/all_gather | solution.py:186
  9.1 9.6 %collective-permute-start.17 = (bf16[48,2560]{1,0:T(8,128)(2,1)S(1)}, bf16[48,2560]{1,0:T(8,128)(2,1)S(1)}, u32[]{:S(2)}, u32[]{:S(2)}) collective-permute-start(bf16[48,2560]{1,0:T(8,128)(2,1)S(1)} %get-tuple-element.114), channel_id=1, source_target_pairs={{0,1},{1,0},{2,3},{3,2},{4,5},{5,4},{6,7},{7,6},{8,9},{9,8},{10,11... | collective-permute-start | bytes 737288 | tf_op jit(solution)/shard_map/cond/branch_2_fun/ppermute | solution.py:176
  19.6 9.3 %copy-start.5 = (bf16[1,1536,128]{2,1,0:T(8,128)(2,1)S(1)}, bf16[1,1536,128]{2,1,0:T(8,128)(2,1)}, u32[]{:S(2)}) copy-start(bf16[1,1536,128]{2,1,0:T(8,128)(2,1)} %get-tuple-element.100) | copy-start | bytes 1179652 | tf_op jit(solution)/shard_map/conditional
  19.6 33.3 %collective-permute-start.18 = (bf16[128,5120]{1,0:T(8,128)(2,1)S(1)}, bf16[128,5120]{1,0:T(8,128)(2,1)}, u32[]{:S(2)}, u32[]{:S(2)}) collective-permute-start(bf16[128,5120]{1,0:T(8,128)(2,1)S(1)} %bitcast.48), channel_id=1, source_target_pairs={{0,128},{128,0},{1,129},{129,1},{2,130},{130,2},{3,131},{131,3},{4... | collective-permute-start | bytes 3932168 | tf_op jit(solution)/shard_map/cond/branch_2_fun/ppermute | solution.py:179
  25.8 25.7 %collective-permute-start.19 = (bf16[128,2560]{1,0:T(8,128)(2,1)S(1)}, bf16[128,2560]{1,0:T(8,128)(2,1)}, u32[]{:S(2)}, u32[]{:S(2)}) collective-permute-start(bf16[128,2560]{1,0:T(8,128)(2,1)S(1)} %get-tuple-element.112), channel_id=1, source_target_pairs={{0,1},{1,0},{2,3},{3,2},{4,5},{5,4},{6,7},{7,6},{8,9},{9,8},{10,11... | collective-permute-start | bytes 1966088 | tf_op jit(solution)/shard_map/cond/branch_2_fun/ppermute | solution.py:176
  29.1 22.4 %copy-start.8 = (bf16[128,2560]{1,0:T(8,128)(2,1)S(1)}, bf16[128,2560]{1,0:T(8,128)(2,1)}, u32[]{:S(2)}) copy-start(bf16[128,2560]{1,0:T(8,128)(2,1)} %get-tuple-element.111) | copy-start | bytes 1966084 | tf_op jit(solution)/shard_map/conditional
  29.1 22.3 %collective-permute-start.16 = (bf16[1536,128]{0,1:T(8,128)(2,1)S(1)}, bf16[1536,128]{0,1:T(8,128)(2,1)S(1)}, u32[]{:S(2)}, u32[]{:S(2)}) collective-permute-start(bf16[1536,128]{0,1:T(8,128)(2,1)S(1)} %bitcast.53), channel_id=1, source_target_pairs={{0,1},{1,0},{2,3},{3,2},{4,5},{5,4},{6,7},{7,6},{8,9},{9,8},{10,11... | collective-permute-start | bytes 1179656 | tf_op jit(solution)/shard_map/cond/branch_2_fun/ppermute | solution.py:176
  133.8 19.3 %collective-permute-start.20 = (bf16[128,2560]{1,0:T(8,128)(2,1)S(1)}, bf16[128,2560]{1,0:T(8,128)(2,1)}, u32[]{:S(2)}, u32[]{:S(2)}) collective-permute-start(bf16[128,2560]{1,0:T(8,128)(2,1)S(1)} %get-tuple-element.61), channel_id=1, source_target_pairs={{0,1},{1,0},{2,3},{3,2},{4,5},{5,4},{6,7},{7,6},{8,9},{9,8},{10,11... | collective-permute-start | bytes 1966088 | tf_op jit(solution)/shard_map/cond/branch_2_fun/ppermute | solution.py:176
  148.1 39.5 %collective-permute-start.21 = (bf16[128,2560]{1,0:T(8,128)(2,1)}, bf16[128,2560]{1,0:T(8,128)(2,1)}, u32[]{:S(2)}, u32[]{:S(2)}) collective-permute-start(bf16[128,2560]{1,0:T(8,128)(2,1)} %get-tuple-element.136), channel_id=1, source_target_pairs={{0,128},{128,0},{1,129},{129,1},{2,130},{130,2},{3,131},{131,3},{4... | collective-permute-start | bytes 1966088 | tf_op jit(solution)/shard_map/cond/branch_2_fun/ppermute | solution.py:179
  153.1 34.6 %collective-permute-start.22 = (bf16[128,2560]{1,0:T(8,128)(2,1)}, bf16[128,2560]{1,0:T(8,128)(2,1)}, u32[]{:S(2)}, u32[]{:S(2)}) collective-permute-start(bf16[128,2560]{1,0:T(8,128)(2,1)} %collective-permute-done.20), channel_id=1, source_target_pairs={{0,128},{128,0},{1,129},{129,1},{2,130},{130,2},{3,131},{131,3},{4... | collective-permute-start | bytes 1966088 | tf_op jit(solution)/shard_map/cond/branch_2_fun/ppermute | solution.py:179
  172.6 15.0 %collective-permute-start.23 = (bf16[1536,128]{1,0:T(8,128)(2,1)S(1)}, bf16[1536,128]{1,0:T(8,128)(2,1)}, u32[]{:S(2)}, u32[]{:S(2)}) collective-permute-start(bf16[1536,128]{1,0:T(8,128)(2,1)S(1)} %get-tuple-element.69), channel_id=1, source_target_pairs={{0,1},{1,0},{2,3},{3,2},{4,5},{5,4},{6,7},{7,6},{8,9},{9,8},{10,11... | collective-permute-start | bytes 1179656 | tf_op jit(solution)/shard_map/cond/branch_2_fun/ppermute | solution.py:176
Sparse Core Ops, SparseCore 0:
  19.7 105.0 all-gather.7

commit v3 on v2

--- a/solution.py
+++ b/solution.py
@@ -12,6 +12,7 @@
 Z = ("zh", "zl")
 PARTNER_AXES = ("core", "yl", "yh")
 VMEM_BYTES = 48 * 1024 * 1024
+SUMMED = 64
 
 
 def products_kernel(
@@ -43,10 +44,10 @@
     def _():
         part_here_ref[...] = total[:, :rows]
         part_there_ref[...] = total[:, rows:].astype(part_there_ref.dtype)
-        squares_ref[0, 0] = jnp.sum(sums[...])
-
-
-def products(heads_t, tokens, weight, blocks=5):
+        squares_ref[...] = jnp.full(squares_ref.shape, jnp.sum(sums[...]), jnp.float32)
+
+
+def products(heads_t, tokens, weight, blocks=4):
     pair_rows, count = heads_t.shape
     rows, width = pair_rows // 2, tokens.shape[1]
     cols = width // blocks
@@ -61,14 +62,14 @@
         out_specs=[
             pl.BlockSpec((rows, cols), lambda i: (0, i)),
             pl.BlockSpec((rows, cols), lambda i: (0, i)),
-            pl.BlockSpec((1, 1), lambda i: (0, 0), memory_space=pltpu.SMEM),
+            pl.BlockSpec((SUMMED, 128), lambda i: (0, 0)),
             pl.BlockSpec((count, rows), lambda i: (0, 0)),
             pl.BlockSpec((count, rows), lambda i: (0, 0)),
         ],
         out_shape=[
             jax.ShapeDtypeStruct((rows, width), jnp.bfloat16),
             jax.ShapeDtypeStruct((rows, width), jnp.bfloat16),
-            jax.ShapeDtypeStruct((1, 1), jnp.float32),
+            jax.ShapeDtypeStruct((SUMMED, 128), jnp.float32),
             jax.ShapeDtypeStruct((count, rows), jnp.float32),
             jax.ShapeDtypeStruct((count, rows), jnp.bfloat16),
         ],
@@ -87,17 +88,18 @@
 
 
 def finish_kernel(
-    multiplier, spot_ref, squares_ref, weight_ref, partner_ref, here_ref, there_ref,
-    partner_here_ref, partner_there_ref, part_ref, from_pair_ref, new_ref, heads_ref,
+    multiplier, spot_ref, weight_ref, partner_ref, here_ref, there_ref,
+    partner_here_ref, partner_there_ref, part_ref, from_pair_ref, squares_ref, new_ref, heads_ref,
 ):
     entries = jnp.float32(4096 * 5120)
     here = pl.program_id(0) == 0
     own = spot_ref[1]
 
     def scale(index):
-        total = jnp.full((8, 128), squares_ref[index], jnp.float32) * (multiplier * multiplier)
+        part = squares_ref[pl.ds(index * (SUMMED // 2), SUMMED // 2), :]
+        total = jnp.sum(part, axis=0, keepdims=True) * (multiplier * multiplier)
         factor = jnp.minimum(1.0, jnp.sqrt(entries) / jnp.sqrt(total))
-        return (step_rate * multiplier * factor)[:1, :1]
+        return (step_rate * multiplier * factor)[:, :1]
 
     def stepped(block_ref, amount, first_ref, second_ref):
         grad = jnp.where(here, first_ref[...], second_ref[...]).astype(jnp.float32)
@@ -112,14 +114,14 @@
     ).astype(heads_ref.dtype)
 
 
-def finish(multiplier, spot, squares, weight, partner, grads, partner_grads, part, from_pair, blocks=2):
+def finish(multiplier, spot, squares, weight, partner, grads, partner_grads, part, from_pair, blocks=1):
     rows, width = weight.shape
     half = width // 2
     cols = half // blocks
     count = part.shape[0]
     piece = count // (2 * blocks)
 
-    def whole(h, i, spot_ref, squares_ref):
+    def whole(h, i, spot_ref):
         return (0, jnp.where(h == 0, spot_ref[0], 1 - spot_ref[0]) * blocks + i)
 
     first = lambda h, i, *_: (0, jnp.where(h == 0, i, blocks - 1))
@@ -129,7 +131,7 @@
     return pl.pallas_call(
         partial(finish_kernel, multiplier),
         grid_spec=pltpu.PrefetchScalarGridSpec(
-            num_scalar_prefetch=2,
+            num_scalar_prefetch=1,
             grid=(2, blocks),
             in_specs=[
                 wide,
@@ -140,6 +142,7 @@
                 pl.BlockSpec((rows, cols), second),
                 pl.BlockSpec((piece, rows), down),
                 pl.BlockSpec((piece, rows), down),
+                pl.BlockSpec((SUMMED, 128), lambda h, i, *_: (0, 0)),
             ],
             out_specs=[wide, pl.BlockSpec((piece, rows), down)],
         ),
@@ -153,7 +156,7 @@
             transcendentals=0,
         ),
         name="finish",
-    )(spot, squares, weight, partner, *grads, *partner_grads, part, from_pair)
+    )(spot, weight, partner, *grads, *partner_grads, part, from_pair, squares)
 
 
 def one_step(level, head_outputs, out_weight, cotangent):
@@ -178,6 +181,9 @@
     def to_partner(block):
         return lax.ppermute(block, partner_axis, PAIR)
 
+    def across(block):
+        return lax.ppermute(block, (partner_axis, "x"), [(0, 3), (1, 2), (2, 1), (3, 0)])
+
     kept = mine(tokens)
     got = swap(other(tokens))
     pair_tokens = jnp.where(
@@ -189,18 +195,15 @@
     weight_pair = jnp.concatenate([mine(weight), swap(other(weight))], 0)
     partner_weight = to_partner(weight)
 
-    gathered, partner_weight = lax.optimization_barrier((gathered, partner_weight))
+    gathered, partner_weight, weight_pair = lax.optimization_barrier(
+        (gathered, partner_weight, weight_pair)
+    )
     here, there, squares, part_here, part_there = products(heads_t, gathered, weight_pair)
+    partner_there = across(there)
     there = swap(there)
     partner_here = to_partner(here)
-    squares = jnp.where(jnp.arange(2) == own, squares[0, 0], 0.0)
-    squares = lax.psum(squares, "zl")
-    squares, there = lax.optimization_barrier((squares, there))
-    partner_there = to_partner(there)
-    squares = lax.psum(squares, "zh")
-    squares, part_there = lax.optimization_barrier((squares, part_there))
     from_pair = swap(part_there)
-    squares = lax.psum(squares, (partner_axis, "x"))
+    squares = lax.all_to_all(squares, (partner_axis, *Z, "x"), 0, 0, tiled=True)
 
     return (
         own, squares, partner_weight, (here, there), (partner_here, partner_there), part_here,

time: 201 us -> 191 us (0.950)
  the two profiles are of different devices: /device:TPU:4 before, /device:TPU:1 now
where the time goes in v3:
time: 191 us; the launch traced here: 190 us
  waiting for transfers between devices  114 us (60%)
  starting transfers between devices  41.6 us (22%)
  Pallas kernels  15.1 us (8%)
  between operations  14.7 us (8%)
  local copies, waits for them, and re-layouts  2.32 us (1%)
  other arithmetic  2.17 us (1%)
    all_gather x1, waiting for transfers between devices, one_step(): gathered = lax.all_gather(pair_tokens, Z, axis=0, tiled=True)  74.9 us
    ppermute x5, waiting for transfers between devices, swap(): return lax.ppermute(block, 'x', PAIR)  22.1 us
    all_to_all x1, waiting for transfers between devices, one_step(): squares = lax.all_to_all(squares, (partner_axis, *Z, 'x'), 0, 0, tiled=True)  17.4 us
    ppermute x5, starting transfers between devices, swap(): return lax.ppermute(block, 'x', PAIR)  15.5 us
    all_to_all x1, starting transfers between devices, one_step(): squares = lax.all_to_all(squares, (partner_axis, *Z, 'x'), 0, 0, tiled=True)  12.2 us
    ppermute x2, starting transfers between devices, to_partner(): return lax.ppermute(block, partner_axis, PAIR)  11.6 us
    pallas_call x1, Pallas kernels, products(): pl.pallas_call(products_kernel, grid=(blocks,), in_specs=[pl.BlockSpec((p...  9.04 us
    pallas_call x1, Pallas kernels, finish(): pl.pallas_call(partial(finish_kernel, multiplier), grid_spec=pltpu.Prefet...  6.09 us
  transfers between devices with their start and end apart: 10, of which 4 were waited for; matrix products, arithmetic and copies ran while one was open for 1% of the time, Pallas kernels for 0%

profile of v3, /device:TPU:1, one launch (start us, length us, event | category | flops | bytes accessed | tf_op | source)
XLA Modules:
  0.0 190.4 jit_solution(2336970885912178384)
XLA Ops:
  7.8 169.6 %conditional.1 = (f32[64,128]{1,0:T(8,128)}, bf16[128,5120]{1,0:T(8,128)(2,1)}, bf16[128,2560]{1,0:T(8,128)(2,1)}, bf16[128,2560]{1,0:T(8,128)(2,1)}, bf16[128,2...) conditional(s32[]{:T(128)} %clamp.3, ...), branch_computations={%region_0.1_spmd, %region_1.2_spmd, %region_2.3_spmd} | conditional | flops 4032937984 | bytes 80020224 | solution.py:216
  7.9 0.0 copy-start.2
  7.9 0.0 all-gather.8.cloned.1.call-start
  7.9 1.2 dynamic-slice_bitcast_fusion.11
  9.1 3.9 %collective-permute-start.17 = (bf16[48,2560]{1,0:T(8,128)(2,1)S(1)}, bf16[48,2560]{1,0:T(8,128)(2,1)S(1)}, u32[]{:S(2)}, u32[]{:S(2)}) collective-permute-start(bf16[48,2560]{1,0:T(8,128)(2,1)S(1)} %get-tuple-element.105), channel_id=1, source_target_pairs={{0,1},{1,0},{2,3},{3,2},{4,5},{5,4},{6,7},{7,6},{8,9},{9,8},{10,11... | collective-permute-start | bytes 737288 | tf_op jit(solution)/shard_map/cond/branch_2_fun/ppermute | solution.py:179
  13.1 3.6 %collective-permute-done.17 = bf16[48,2560]{1,0:T(8,128)(2,1)S(1)} collective-permute-done((bf16[48,2560]{1,0:T(8,128)(2,1)S(1)}, bf16[48,2560]{1,0:T(8,128)(2,1)S(1)}, u32[]{:S(2)}, u32[]{:S(2)}) %collective-permute-start.17) | collective-permute-done | bytes 245792 | tf_op jit(solution)/shard_map/cond/branch_2_fun/ppermute | solution.py:179
  16.6 0.9 maximum_select_fusion.2
  17.5 0.0 all-gather.8.cloned.1.call-update
  17.6 7.0 %collective-permute-start.18 = (bf16[128,5120]{1,0:T(8,128)(2,1)S(1)}, bf16[128,5120]{1,0:T(8,128)(2,1)}, u32[]{:S(2)}, u32[]{:S(2)}) collective-permute-start(bf16[128,5120]{1,0:T(8,128)(2,1)S(1)} %bitcast.59), channel_id=1, source_target_pairs={{0,128},{128,0},{1,129},{129,1},{2,130},{130,2},{3,131},{131,3},{4... | collective-permute-start | bytes 3932168 | tf_op jit(solution)/shard_map/cond/branch_2_fun/ppermute | solution.py:182
  24.5 0.9 dynamic-slice_bitcast_fusion.9
  25.5 3.1 %collective-permute-start.19 = (bf16[128,2560]{1,0:T(8,128)(2,1)S(1)}, bf16[128,2560]{1,0:T(8,128)(2,1)}, u32[]{:S(2)}, u32[]{:S(2)}) collective-permute-start(bf16[128,2560]{1,0:T(8,128)(2,1)S(1)} %get-tuple-element.103), channel_id=1, source_target_pairs={{0,1},{1,0},{2,3},{3,2},{4,5},{5,4},{6,7},{7,6},{8,9},{9,8},{10,11... | collective-permute-start | bytes 1966088 | tf_op jit(solution)/shard_map/cond/branch_2_fun/ppermute | solution.py:179
  28.6 0.2 copy.14
  28.8 0.0 copy-start.8
  28.8 2.3 %collective-permute-start.16 = (bf16[1536,128]{0,1:T(8,128)(2,1)S(1)}, bf16[1536,128]{0,1:T(8,128)(2,1)S(1)}, u32[]{:S(2)}, u32[]{:S(2)}) collective-permute-start(bf16[1536,128]{0,1:T(8,128)(2,1)S(1)} %bitcast.64), channel_id=1, source_target_pairs={{0,1},{1,0},{2,3},{3,2},{4,5},{5,4},{6,7},{7,6},{8,9},{9,8},{10,11... | collective-permute-start | bytes 1179656 | tf_op jit(solution)/shard_map/cond/branch_2_fun/ppermute | solution.py:179
  31.1 18.5 %collective-permute-done.16 = bf16[1536,128]{0,1:T(8,128)(2,1)S(1)} collective-permute-done((bf16[1536,128]{0,1:T(8,128)(2,1)S(1)}, bf16[1536,128]{0,1:T(8,128)(2,1)S(1)}, u32[]{:S(2)}, u32[]{:S(2)}) %collective-permute-start.16) | collective-permute-done | bytes 393248 | tf_op jit(solution)/shard_map/cond/branch_2_fun/ppermute | solution.py:179
  49.6 0.1 maximum_bitcast_fusion.2.heads_ref
  49.6 0.0 collective-permute-done.19
  49.7 1.2 pad_maximum_fusion.2.weight_ref
  50.8 0.0 collective-permute-done.18
  50.8 74.9 %all-gather.8.cloned.1.call-done.tokens_ref = bf16[1536,2560]{1,0:T(8,128)(2,1)} async-done(((bf16[96,2560]{1,0:T(8,128)(2,1)}), bf16[1536,2560]{1,0:T(8,128)(2,1)}) %all-gather.8.cloned.1.call-update) | async-done | bytes 7864336 | tf_op jit(solution)/shard_map/cond/branch_2_fun/all_gather | solution.py:192
  125.7 9.0 %products.5 = (bf16[128,2560]{1,0:T(8,128)(2,1)}, bf16[128,2560]{1,0:T(8,128)(2,1)S(1)}, f32[64,128]{1,0:T(8,128)}, f32[1536,128]{1,0:T(8,128)}, bf16[1536,128]{1,0:T(8,128)(2,1)S(1)}) custom-call(bf16[256,1536]{1,0:T(8,128)(2,1)S(1)} %maximum_bitcast_fusion.2.heads_ref, bf16[1536,2560]{1,0:T(8,128)(2,1)} %all-gather.8.cloned.1.call-done.tokens_ref, ...), custom_call_target="tpu_custom_call" | custom-call | flops 4026531840 | bytes 13369344 | tf_op jit(solution)/shard_map/cond/branch_2_fun/products/pallas_call | solution.py:54
  134.8 3.1 %collective-permute-start.20 = (bf16[128,2560]{1,0:T(8,128)(2,1)S(1)}, bf16[128,2560]{1,0:T(8,128)(2,1)}, u32[]{:S(2)}, u32[]{:S(2)}) collective-permute-start(bf16[128,2560]{1,0:T(8,128)(2,1)S(1)} %get-tuple-element.49), channel_id=1, source_target_pairs={{0,1},{1,0},{2,3},{3,2},{4,5},{5,4},{6,7},{7,6},{8,9},{9,8},{10,11... | collective-permute-start | bytes 1966088 | tf_op jit(solution)/shard_map/cond/branch_2_fun/ppermute | solution.py:179
  137.9 4.6 %collective-permute-start.21 = (bf16[128,2560]{1,0:T(8,128)(2,1)}, bf16[128,2560]{1,0:T(8,128)(2,1)}, u32[]{:S(2)}, u32[]{:S(2)}) collective-permute-start(bf16[128,2560]{1,0:T(8,128)(2,1)} %get-tuple-element.126), channel_id=1, source_target_pairs={{0,128},{128,0},{1,129},{129,1},{2,130},{130,2},{3,131},{131,3},{4... | collective-permute-start | bytes 1966088 | tf_op jit(solution)/shard_map/cond/branch_2_fun/ppermute | solution.py:182
  142.5 2.1 %collective-permute-start.22 = (bf16[128,2560]{1,0:T(8,128)(2,1)S(1)}, bf16[128,2560]{1,0:T(8,128)(2,1)}, u32[]{:S(2)}, u32[]{:S(2)}) collective-permute-start(bf16[128,2560]{1,0:T(8,128)(2,1)S(1)} %get-tuple-element.49), channel_id=1, source_target_pairs={{0,129},{1,128},{128,1},{129,0},{2,131},{3,130},{130,3},{131,2},{4... | collective-permute-start | bytes 1966088 | tf_op jit(solution)/shard_map/cond/branch_2_fun/ppermute | solution.py:185
  144.7 3.1 %collective-permute-start.23 = (bf16[1536,128]{1,0:T(8,128)(2,1)S(1)}, bf16[1536,128]{1,0:T(8,128)(2,1)}, u32[]{:S(2)}, u32[]{:S(2)}) collective-permute-start(bf16[1536,128]{1,0:T(8,128)(2,1)S(1)} %get-tuple-element.51), channel_id=1, source_target_pairs={{0,1},{1,0},{2,3},{3,2},{4,5},{5,4},{6,7},{7,6},{8,9},{9,8},{10,11... | collective-permute-start | bytes 1179656 | tf_op jit(solution)/shard_map/cond/branch_2_fun/ppermute | solution.py:179
  147.8 12.2 %all-to-all-start.2 = ((f32[64,1,128]{2,1,0:T(1,128)}), f32[64,1,128]{2,1,0:T(1,128)}, u32[]{:S(2)}, u32[]{:S(2)}) async-start(f32[64,1,128]{2,1,0:T(1,128)} %bitcast.32), calls=%async_computation.2 | async-start | bytes 65536 | tf_op jit(solution)/shard_map/cond/branch_2_fun/all_to_all | solution.py:206
  160.0 17.4 %all-to-all-done.2 = f32[64,1,128]{2,1,0:T(1,128)} async-done(((f32[64,1,128]{2,1,0:T(1,128)}), f32[64,1,128]{2,1,0:T(1,128)}, u32[]{:S(2)}, u32[]{:S(2)}) %all-to-all-start.2) | async-done | bytes 32800 | tf_op jit(solution)/shard_map/cond/branch_2_fun/all_to_all | solution.py:206
  177.4 0.0 collective-permute-done.20
  177.4 0.0 collective-permute-done.21
  177.4 0.0 collective-permute-done.22
  177.4 0.1 pad_add_fusion.spot_ref
  177.5 6.1 %finish.1 = (bf16[128,5120]{1,0:T(8,128)(2,1)}, bf16[1536,128]{1,0:T(8,128)(2,1)}) custom-call(s32[2]{0:T(128)S(1)} %pad_add_fusion.spot_ref, bf16[128,5120]{1,0:T(8,128)(2,1)} %bitcast.56, bf16[128,5120]{1,0:T(8,128)(2,1)} %get-tuple-element.66.partner_ref, bf16[128,2560]{1,0:T(8,128)(2,1)} %get-tuple-element.67.here_ref, ...), custom_call_target="tpu_custom_call" | custom-call | flops 5242880 | bytes 8126464 | tf_op jit(solution)/shard_map/finish/pallas_call | solution.py:131
  (5 shorter events, 0.0 us)
Async XLA Ops:
  7.9 9.7 %copy-start.2 = (bf16[1,128,5120]{2,1,0:T(8,128)(2,1)S(1)}, bf16[1,128,5120]{2,1,0:T(8,128)(2,1)}, u32[]{:S(2)}) copy-start(bf16[1,128,5120]{2,1,0:T(8,128)(2,1)} %get-tuple-element.43) | copy-start | bytes 3932164 | tf_op jit(solution)/shard_map/cond
  7.9 117.9 %all-gather.8.cloned.1.call-start = ((), (), s32[]{:S(2)}) async-start(), calls=%async_computation.5 | async-start | bytes 8355840 | tf_op jit(solution)/shard_map/cond/branch_2_fun/all_gather | solution.py:192
  9.1 7.5 %collective-permute-start.17 = (bf16[48,2560]{1,0:T(8,128)(2,1)S(1)}, bf16[48,2560]{1,0:T(8,128)(2,1)S(1)}, u32[]{:S(2)}, u32[]{:S(2)}) collective-permute-start(bf16[48,2560]{1,0:T(8,128)(2,1)S(1)} %get-tuple-element.105), channel_id=1, source_target_pairs={{0,1},{1,0},{2,3},{3,2},{4,5},{5,4},{6,7},{7,6},{8,9},{9,8},{10,11... | collective-permute-start | bytes 737288 | tf_op jit(solution)/shard_map/cond/branch_2_fun/ppermute | solution.py:179
  17.5 11.1 %copy-start.5 = (bf16[1,1536,128]{2,1,0:T(8,128)(2,1)S(1)}, bf16[1,1536,128]{2,1,0:T(8,128)(2,1)}, u32[]{:S(2)}) copy-start(bf16[1,1536,128]{2,1,0:T(8,128)(2,1)} %get-tuple-element.91) | copy-start | bytes 1179652 | tf_op jit(solution)/shard_map/cond
  17.6 33.3 %collective-permute-start.18 = (bf16[128,5120]{1,0:T(8,128)(2,1)S(1)}, bf16[128,5120]{1,0:T(8,128)(2,1)}, u32[]{:S(2)}, u32[]{:S(2)}) collective-permute-start(bf16[128,5120]{1,0:T(8,128)(2,1)S(1)} %bitcast.59), channel_id=1, source_target_pairs={{0,128},{128,0},{1,129},{129,1},{2,130},{130,2},{3,131},{131,3},{4... | collective-permute-start | bytes 3932168 | tf_op jit(solution)/shard_map/cond/branch_2_fun/ppermute | solution.py:182
  25.5 24.2 %collective-permute-start.19 = (bf16[128,2560]{1,0:T(8,128)(2,1)S(1)}, bf16[128,2560]{1,0:T(8,128)(2,1)}, u32[]{:S(2)}, u32[]{:S(2)}) collective-permute-start(bf16[128,2560]{1,0:T(8,128)(2,1)S(1)} %get-tuple-element.103), channel_id=1, source_target_pairs={{0,1},{1,0},{2,3},{3,2},{4,5},{5,4},{6,7},{7,6},{8,9},{9,8},{10,11... | collective-permute-start | bytes 1966088 | tf_op jit(solution)/shard_map/cond/branch_2_fun/ppermute | solution.py:179
  28.8 20.9 %copy-start.8 = (bf16[128,2560]{1,0:T(8,128)(2,1)S(1)}, bf16[128,2560]{1,0:T(8,128)(2,1)}, u32[]{:S(2)}) copy-start(bf16[128,2560]{1,0:T(8,128)(2,1)} %get-tuple-element.102) | copy-start | bytes 1966084 | tf_op jit(solution)/shard_map/cond
  28.8 20.8 %collective-permute-start.16 = (bf16[1536,128]{0,1:T(8,128)(2,1)S(1)}, bf16[1536,128]{0,1:T(8,128)(2,1)S(1)}, u32[]{:S(2)}, u32[]{:S(2)}) collective-permute-start(bf16[1536,128]{0,1:T(8,128)(2,1)S(1)} %bitcast.64), channel_id=1, source_target_pairs={{0,1},{1,0},{2,3},{3,2},{4,5},{5,4},{6,7},{7,6},{8,9},{9,8},{10,11... | collective-permute-start | bytes 1179656 | tf_op jit(solution)/shard_map/cond/branch_2_fun/ppermute | solution.py:179
  134.8 42.6 %collective-permute-start.20 = (bf16[128,2560]{1,0:T(8,128)(2,1)S(1)}, bf16[128,2560]{1,0:T(8,128)(2,1)}, u32[]{:S(2)}, u32[]{:S(2)}) collective-permute-start(bf16[128,2560]{1,0:T(8,128)(2,1)S(1)} %get-tuple-element.49), channel_id=1, source_target_pairs={{0,1},{1,0},{2,3},{3,2},{4,5},{5,4},{6,7},{7,6},{8,9},{9,8},{10,11... | collective-permute-start | bytes 1966088 | tf_op jit(solution)/shard_map/cond/branch_2_fun/ppermute | solution.py:179
  137.9 39.5 %collective-permute-start.21 = (bf16[128,2560]{1,0:T(8,128)(2,1)}, bf16[128,2560]{1,0:T(8,128)(2,1)}, u32[]{:S(2)}, u32[]{:S(2)}) collective-permute-start(bf16[128,2560]{1,0:T(8,128)(2,1)} %get-tuple-element.126), channel_id=1, source_target_pairs={{0,128},{128,0},{1,129},{129,1},{2,130},{130,2},{3,131},{131,3},{4... | collective-permute-start | bytes 1966088 | tf_op jit(solution)/shard_map/cond/branch_2_fun/ppermute | solution.py:182
  142.5 34.9 %collective-permute-start.22 = (bf16[128,2560]{1,0:T(8,128)(2,1)S(1)}, bf16[128,2560]{1,0:T(8,128)(2,1)}, u32[]{:S(2)}, u32[]{:S(2)}) collective-permute-start(bf16[128,2560]{1,0:T(8,128)(2,1)S(1)} %get-tuple-element.49), channel_id=1, source_target_pairs={{0,129},{1,128},{128,1},{129,0},{2,131},{3,130},{130,3},{131,2},{4... | collective-permute-start | bytes 1966088 | tf_op jit(solution)/shard_map/cond/branch_2_fun/ppermute | solution.py:185
  144.7 32.7 %collective-permute-start.23 = (bf16[1536,128]{1,0:T(8,128)(2,1)S(1)}, bf16[1536,128]{1,0:T(8,128)(2,1)}, u32[]{:S(2)}, u32[]{:S(2)}) collective-permute-start(bf16[1536,128]{1,0:T(8,128)(2,1)S(1)} %get-tuple-element.51), channel_id=1, source_target_pairs={{0,1},{1,0},{2,3},{3,2},{4,5},{5,4},{6,7},{7,6},{8,9},{9,8},{10,11... | collective-permute-start | bytes 1179656 | tf_op jit(solution)/shard_map/cond/branch_2_fun/ppermute | solution.py:179
  147.8 29.6 %all-to-all-start.2 = ((f32[64,1,128]{2,1,0:T(1,128)}), f32[64,1,128]{2,1,0:T(1,128)}, u32[]{:S(2)}, u32[]{:S(2)}) async-start(f32[64,1,128]{2,1,0:T(1,128)} %bitcast.32), calls=%async_computation.2 | async-start | bytes 65536 | tf_op jit(solution)/shard_map/cond/branch_2_fun/all_to_all | solution.py:206
Sparse Core Ops, SparseCore 0:
  17.7 108.0 all-gather.7

commit v4 on v3

--- a/solution.py
+++ b/solution.py
@@ -15,76 +15,93 @@
 SUMMED = 64
 
 
-def products_kernel(
-    heads_ref, tokens_ref, weight_ref, here_ref, there_ref, squares_ref, part_here_ref,
-    part_there_ref, total, sums,
-):
+def gradient_kernel(heads_ref, tokens_ref, here_ref, there_ref, squares_ref, sums):
     rows = here_ref.shape[0]
     step, last = pl.program_id(0), pl.num_programs(0) - 1
-    block = tokens_ref[...]
-    grad = jnp.dot(heads_ref[...], block, preferred_element_type=jnp.float32)
+    grad = jnp.dot(heads_ref[...], tokens_ref[...], preferred_element_type=jnp.float32)
     here_ref[...] = grad[:rows].astype(here_ref.dtype)
     there_ref[...] = grad[rows:].astype(there_ref.dtype)
-    part = lax.dot_general(
-        block, weight_ref[...], (((1,), (1,)), ((), ())), preferred_element_type=jnp.float32
-    )
     column_sums = jnp.sum(grad * grad, axis=0, keepdims=True)
 
     @pl.when(step == 0)
     def _():
-        total[...] = part
         sums[...] = column_sums
 
     @pl.when(step > 0)
     def _():
-        total[...] += part
         sums[...] += column_sums
 
     @pl.when(step == last)
     def _():
-        part_here_ref[...] = total[:, :rows]
-        part_there_ref[...] = total[:, rows:].astype(part_there_ref.dtype)
         squares_ref[...] = jnp.full(squares_ref.shape, jnp.sum(sums[...]), jnp.float32)
 
 
-def products(heads_t, tokens, weight, blocks=4):
+def gradient(heads_t, tokens, blocks=2):
     pair_rows, count = heads_t.shape
     rows, width = pair_rows // 2, tokens.shape[1]
     cols = width // blocks
     return pl.pallas_call(
-        products_kernel,
+        gradient_kernel,
         grid=(blocks,),
         in_specs=[
             pl.BlockSpec((pair_rows, count), lambda i: (0, 0)),
             pl.BlockSpec((count, cols), lambda i: (0, i)),
-            pl.BlockSpec((pair_rows, cols), lambda i: (0, i)),
         ],
         out_specs=[
             pl.BlockSpec((rows, cols), lambda i: (0, i)),
             pl.BlockSpec((rows, cols), lambda i: (0, i)),
             pl.BlockSpec((SUMMED, 128), lambda i: (0, 0)),
-            pl.BlockSpec((count, rows), lambda i: (0, 0)),
-            pl.BlockSpec((count, rows), lambda i: (0, 0)),
         ],
         out_shape=[
             jax.ShapeDtypeStruct((rows, width), jnp.bfloat16),
             jax.ShapeDtypeStruct((rows, width), jnp.bfloat16),
             jax.ShapeDtypeStruct((SUMMED, 128), jnp.float32),
+        ],
+        scratch_shapes=[pltpu.VMEM((1, cols), jnp.float32)],
+        compiler_params=pltpu.CompilerParams(vmem_limit_bytes=VMEM_BYTES),
+        cost_estimate=pl.CostEstimate(
+            flops=2 * pair_rows * count * width,
+            bytes_accessed=2 * (count * width + pair_rows * width + pair_rows * count),
+            transcendentals=0,
+        ),
+        name="gradient",
+    )(heads_t, tokens)
+
+
+def head_parts_kernel(tokens_ref, weight_ref, here_ref, there_ref):
+    rows = here_ref.shape[1]
+    part = lax.dot_general(
+        tokens_ref[...], weight_ref[...], (((1,), (1,)), ((), ())),
+        preferred_element_type=jnp.float32,
+    )
+    here_ref[...] = part[:, :rows]
+    there_ref[...] = part[:, rows:].astype(there_ref.dtype)
+
+
+def head_parts(tokens, weight, blocks=2):
+    count, width = tokens.shape
+    pair_rows = weight.shape[0]
+    rows, piece = pair_rows // 2, count // blocks
+    return pl.pallas_call(
+        head_parts_kernel,
+        grid=(blocks,),
+        in_specs=[
+            pl.BlockSpec((piece, width), lambda i: (i, 0)),
+            pl.BlockSpec((pair_rows, width), lambda i: (0, 0)),
+        ],
+        out_specs=[pl.BlockSpec((piece, rows), lambda i: (i, 0))] * 2,
+        out_shape=[
             jax.ShapeDtypeStruct((count, rows), jnp.float32),
             jax.ShapeDtypeStruct((count, rows), jnp.bfloat16),
         ],
-        scratch_shapes=[
-            pltpu.VMEM((count, pair_rows), jnp.float32),
-            pltpu.VMEM((1, cols), jnp.float32),
-        ],
         compiler_params=pltpu.CompilerParams(vmem_limit_bytes=VMEM_BYTES),
         cost_estimate=pl.CostEstimate(
-            flops=4 * pair_rows * count * width,
-            bytes_accessed=2 * (count * width + 3 * pair_rows * width + 4 * count * rows),
+            flops=2 * pair_rows * count * width,
+            bytes_accessed=2 * (count * width + pair_rows * width + 3 * rows * count),
             transcendentals=0,
         ),
-        name="products",
-    )(heads_t, tokens, weight)
+        name="head_parts",
+    )(tokens, weight)
 
 
 def finish_kernel(
@@ -92,7 +109,6 @@
     partner_here_ref, partner_there_ref, part_ref, from_pair_ref, squares_ref, new_ref, heads_ref,
 ):
     entries = jnp.float32(4096 * 5120)
-    here = pl.program_id(0) == 0
     own = spot_ref[1]
 
     def scale(index):
@@ -101,14 +117,23 @@
         factor = jnp.minimum(1.0, jnp.sqrt(entries) / jnp.sqrt(total))
         return (step_rate * multiplier * factor)[:, :1]
 
-    def stepped(block_ref, amount, first_ref, second_ref):
-        grad = jnp.where(here, first_ref[...], second_ref[...]).astype(jnp.float32)
-        new = block_ref[...].astype(jnp.float32) - amount * grad
-        return new.astype(jnp.bfloat16).astype(jnp.float32)
-
-    mine = stepped(weight_ref, scale(own), here_ref, there_ref)
-    theirs = stepped(partner_ref, scale(1 - own), partner_here_ref, partner_there_ref)
-    new_ref[...] = ((mine + theirs) * 0.5).astype(new_ref.dtype)
+    def stepped(block_ref, amount, grad_ref):
+        new = block_ref[...].astype(jnp.float32) - amount * grad_ref[...].astype(jnp.float32)
+        return new.astype(jnp.bfloat16)
+
+    def average(grad_ref, partner_grad_ref):
+        mine = stepped(weight_ref, scale(own), grad_ref)
+        theirs = stepped(partner_ref, scale(1 - own), partner_grad_ref)
+        new_ref[...] = (mine + theirs) * jnp.bfloat16(0.5)
+
+    @pl.when(pl.program_id(0) == 0)
+    def _():
+        average(here_ref, partner_here_ref)
+
+    @pl.when(pl.program_id(0) == 1)
+    def _():
+        average(there_ref, partner_there_ref)
+
     heads_ref[...] = (
         multiplier * (part_ref[...] + from_pair_ref[...].astype(jnp.float32))
     ).astype(heads_ref.dtype)
@@ -198,11 +223,13 @@
     gathered, partner_weight, weight_pair = lax.optimization_barrier(
         (gathered, partner_weight, weight_pair)
     )
-    here, there, squares, part_here, part_there = products(heads_t, gathered, weight_pair)
+    here, there, squares = gradient(heads_t, gathered)
     partner_there = across(there)
     there = swap(there)
     partner_here = to_partner(here)
+    part_here, part_there = head_parts(gathered, weight_pair)
     from_pair = swap(part_there)
+    squares, part_there = lax.optimization_barrier((squares, part_there))
     squares = lax.all_to_all(squares, (partner_axis, *Z, "x"), 0, 0, tiled=True)
 
     return (

time: 191 us -> 192 us (level)
    pallas_call x1 -> x2, Pallas kernels: 9.04 us -> 10 us  [the longest x1 5.46 us: gradient(): pl.pallas_call(gradient_kernel, grid=(blocks,), in_specs=[pl.BlockSpec((p...]
  transfers between devices with their start and end apart: 10 -> 10, of which waited for: 4 -> 4; matrix products, arithmetic and copies ran while one was open for 1% -> 1% of each run, Pallas kernels for 0% -> 2%
where the time goes in v4:
time: 192 us; the launch traced here: 191 us
  waiting for transfers between devices  114 us (59%)
  starting transfers between devices  41.5 us (22%)
  Pallas kernels  15.6 us (8%)
  between operations  14.7 us (8%)
  local copies, waits for them, and re-layouts  2.57 us (1%)
  other arithmetic  2.17 us (1%)
    all_gather x1, waiting for transfers between devices, one_step(): gathered = lax.all_gather(pair_tokens, Z, axis=0, tiled=True)  74.4 us
    ppermute x5, waiting for transfers between devices, swap(): return lax.ppermute(block, 'x', PAIR)  22.3 us
    all_to_all x1, waiting for transfers between devices, one_step(): squares = lax.all_to_all(squares, (partner_axis, *Z, 'x'), 0, 0, tiled=True)  17.1 us
    ppermute x5, starting transfers between devices, swap(): return lax.ppermute(block, 'x', PAIR)  14.6 us
    all_to_all x1, starting transfers between devices, one_step(): squares = lax.all_to_all(squares, (partner_axis, *Z, 'x'), 0, 0, tiled=True)  12.2 us
    ppermute x2, starting transfers between devices, to_partner(): return lax.ppermute(block, partner_axis, PAIR)  11.6 us
    pallas_call x1, Pallas kernels, finish(): pl.pallas_call(partial(finish_kernel, multiplier), grid_spec=pltpu.Prefet...  5.51 us
    pallas_call x1, Pallas kernels, gradient(): pl.pallas_call(gradient_kernel, grid=(blocks,), in_specs=[pl.BlockSpec((p...  5.46 us
  transfers between devices with their start and end apart: 10, of which 4 were waited for; matrix products, arithmetic and copies ran while one was open for 1% of the time, Pallas kernels for 2%

profile of v4, /device:TPU:1, one launch (start us, length us, event | category | flops | bytes accessed | tf_op | source)
XLA Modules:
  0.0 190.6 jit_solution(1950080759830250566)
XLA Ops:
  7.8 170.3 %conditional.1 = (f32[64,128]{1,0:T(8,128)}, bf16[128,5120]{1,0:T(8,128)(2,1)}, bf16[128,2560]{1,0:T(8,128)(2,1)}, bf16[128,2560]{1,0:T(8,128)(2,1)}, bf16[128,2...) conditional(s32[]{:T(128)} %clamp.3, ...), branch_computations={%region_0.1_spmd, %region_1.2_spmd, %region_2.3_spmd} | conditional | flops 4032937984 | bytes 84345568 | solution.py:243
  7.9 0.0 copy-start.2
  7.9 0.0 all-gather.8.cloned.1.call-start
  7.9 1.2 dynamic-slice_bitcast_fusion.11
  9.1 3.9 %collective-permute-start.17 = (bf16[48,2560]{1,0:T(8,128)(2,1)S(1)}, bf16[48,2560]{1,0:T(8,128)(2,1)S(1)}, u32[]{:S(2)}, u32[]{:S(2)}) collective-permute-start(bf16[48,2560]{1,0:T(8,128)(2,1)S(1)} %get-tuple-element.108), channel_id=1, source_target_pairs={{0,1},{1,0},{2,3},{3,2},{4,5},{5,4},{6,7},{7,6},{8,9},{9,8},{10,11... | collective-permute-start | bytes 737288 | tf_op jit(solution)/shard_map/cond/branch_2_fun/ppermute | solution.py:204
  13.1 3.6 %collective-permute-done.17 = bf16[48,2560]{1,0:T(8,128)(2,1)S(1)} collective-permute-done((bf16[48,2560]{1,0:T(8,128)(2,1)S(1)}, bf16[48,2560]{1,0:T(8,128)(2,1)S(1)}, u32[]{:S(2)}, u32[]{:S(2)}) %collective-permute-start.17) | collective-permute-done | bytes 245792 | tf_op jit(solution)/shard_map/cond/branch_2_fun/ppermute | solution.py:204
  16.7 0.9 maximum_select_fusion.2
  17.5 0.0 all-gather.8.cloned.1.call-update
  17.6 7.0 %collective-permute-start.18 = (bf16[128,5120]{1,0:T(8,128)(2,1)S(1)}, bf16[128,5120]{1,0:T(8,128)(2,1)}, u32[]{:S(2)}, u32[]{:S(2)}) collective-permute-start(bf16[128,5120]{1,0:T(8,128)(2,1)S(1)} %bitcast.59), channel_id=1, source_target_pairs={{0,128},{128,0},{1,129},{129,1},{2,130},{130,2},{3,131},{131,3},{4... | collective-permute-start | bytes 3932168 | tf_op jit(solution)/shard_map/cond/branch_2_fun/ppermute | solution.py:207
  24.5 1.2 dynamic-slice_bitcast_fusion.9
  25.7 3.1 %collective-permute-start.19 = (bf16[128,2560]{1,0:T(8,128)(2,1)}, bf16[128,2560]{1,0:T(8,128)(2,1)}, u32[]{:S(2)}, u32[]{:S(2)}) collective-permute-start(bf16[128,2560]{1,0:T(8,128)(2,1)} %get-tuple-element.106), channel_id=1, source_target_pairs={{0,1},{1,0},{2,3},{3,2},{4,5},{5,4},{6,7},{7,6},{8,9},{9,8},{10,11... | collective-permute-start | bytes 1966088 | tf_op jit(solution)/shard_map/cond/branch_2_fun/ppermute | solution.py:204
  28.8 0.2 copy.14
  29.0 0.0 copy-start.8
  29.0 2.3 %collective-permute-start.16 = (bf16[1536,128]{0,1:T(8,128)(2,1)S(1)}, bf16[1536,128]{0,1:T(8,128)(2,1)S(1)}, u32[]{:S(2)}, u32[]{:S(2)}) collective-permute-start(bf16[1536,128]{0,1:T(8,128)(2,1)S(1)} %bitcast.64), channel_id=1, source_target_pairs={{0,1},{1,0},{2,3},{3,2},{4,5},{5,4},{6,7},{7,6},{8,9},{9,8},{10,11... | collective-permute-start | bytes 1179656 | tf_op jit(solution)/shard_map/cond/branch_2_fun/ppermute | solution.py:204
  31.3 18.7 %collective-permute-done.16 = bf16[1536,128]{0,1:T(8,128)(2,1)S(1)} collective-permute-done((bf16[1536,128]{0,1:T(8,128)(2,1)S(1)}, bf16[1536,128]{0,1:T(8,128)(2,1)S(1)}, u32[]{:S(2)}, u32[]{:S(2)}) %collective-permute-start.16) | collective-permute-done | bytes 393248 | tf_op jit(solution)/shard_map/cond/branch_2_fun/ppermute | solution.py:204
  50.0 0.1 maximum_bitcast_fusion.2.heads_ref
  50.1 0.0 collective-permute-done.19
  50.1 1.2 pad_maximum_fusion.2.weight_ref
  51.3 0.0 collective-permute-done.18
  51.3 74.4 %all-gather.8.cloned.1.call-done.tokens_ref = bf16[1536,2560]{1,0:T(8,128)(2,1)} async-done(((bf16[96,2560]{1,0:T(8,128)(2,1)}), bf16[1536,2560]{1,0:T(8,128)(2,1)}) %all-gather.8.cloned.1.call-update) | async-done | bytes 7864336 | tf_op jit(solution)/shard_map/cond/branch_2_fun/all_gather | solution.py:217
  125.7 5.5 %gradient.5 = (bf16[128,2560]{1,0:T(8,128)(2,1)}, bf16[128,2560]{1,0:T(8,128)(2,1)S(1)}, f32[64,128]{1,0:T(8,128)}) custom-call(bf16[256,1536]{1,0:T(8,128)(2,1)S(1)} %maximum_bitcast_fusion.2.heads_ref, bf16[1536,2560]{1,0:T(8,128)(2,1)} %all-gather.8.cloned.1.call-done.tokens_ref), custom_call_target="tpu_custom_call" | custom-call | flops 2013265920 | bytes 9961472 | tf_op jit(solution)/shard_map/cond/branch_2_fun/gradient/pallas_call | solution.py:43
  131.2 4.6 %collective-permute-start.21 = (bf16[128,2560]{1,0:T(8,128)(2,1)}, bf16[128,2560]{1,0:T(8,128)(2,1)}, u32[]{:S(2)}, u32[]{:S(2)}) collective-permute-start(bf16[128,2560]{1,0:T(8,128)(2,1)} %get-tuple-element.129), channel_id=1, source_target_pairs={{0,128},{128,0},{1,129},{129,1},{2,130},{130,2},{3,131},{131,3},{4... | collective-permute-start | bytes 1966088 | tf_op jit(solution)/shard_map/cond/branch_2_fun/ppermute | solution.py:207
  135.8 3.0 %collective-permute-start.22 = (bf16[128,2560]{1,0:T(8,128)(2,1)S(1)}, bf16[128,2560]{1,0:T(8,128)(2,1)}, u32[]{:S(2)}, u32[]{:S(2)}) collective-permute-start(bf16[128,2560]{1,0:T(8,128)(2,1)S(1)} %get-tuple-element.53), channel_id=1, source_target_pairs={{0,129},{1,128},{128,1},{129,0},{2,131},{3,130},{130,3},{131,2},{4... | collective-permute-start | bytes 1966088 | tf_op jit(solution)/shard_map/cond/branch_2_fun/ppermute | solution.py:210
  138.9 2.2 %collective-permute-start.20 = (bf16[128,2560]{1,0:T(8,128)(2,1)S(1)}, bf16[128,2560]{1,0:T(8,128)(2,1)}, u32[]{:S(2)}, u32[]{:S(2)}) collective-permute-start(bf16[128,2560]{1,0:T(8,128)(2,1)S(1)} %get-tuple-element.53), channel_id=1, source_target_pairs={{0,1},{1,0},{2,3},{3,2},{4,5},{5,4},{6,7},{7,6},{8,9},{9,8},{10,11... | collective-permute-start | bytes 1966088 | tf_op jit(solution)/shard_map/cond/branch_2_fun/ppermute | solution.py:204
  141.1 4.6 %head_parts.5 = (f32[1536,128]{1,0:T(8,128)S(1)}, bf16[1536,128]{1,0:T(8,128)(2,1)S(1)}) custom-call(bf16[1536,2560]{1,0:T(8,128)(2,1)} %all-gather.8.cloned.1.call-done.tokens_ref, bf16[256,2560]{1,0:T(8,128)(2,1)S(1)} %pad_maximum_fusion.2.weight_ref), custom_call_target="tpu_custom_call" | custom-call | flops 2013265920 | bytes 10354688 | tf_op jit(solution)/shard_map/cond/branch_2_fun/head_parts/pallas_call | solution.py:85
  145.7 3.1 %collective-permute-start.23 = (bf16[1536,128]{1,0:T(8,128)(2,1)S(1)}, bf16[1536,128]{1,0:T(8,128)(2,1)}, u32[]{:S(2)}, u32[]{:S(2)}) collective-permute-start(bf16[1536,128]{1,0:T(8,128)(2,1)S(1)} %get-tuple-element.49), channel_id=1, source_target_pairs={{0,1},{1,0},{2,3},{3,2},{4,5},{5,4},{6,7},{7,6},{8,9},{9,8},{10,11... | collective-permute-start | bytes 1179656 | tf_op jit(solution)/shard_map/cond/branch_2_fun/ppermute | solution.py:204
  148.8 12.2 %all-to-all-start.2 = ((f32[64,1,128]{2,1,0:T(1,128)}), f32[64,1,128]{2,1,0:T(1,128)}, u32[]{:S(2)}, u32[]{:S(2)}) async-start(f32[64,1,128]{2,1,0:T(1,128)} %bitcast.32), calls=%async_computation.2 | async-start | bytes 65536 | tf_op jit(solution)/shard_map/cond/branch_2_fun/all_to_all | solution.py:233
  161.0 17.1 %all-to-all-done.2 = f32[64,1,128]{2,1,0:T(1,128)} async-done(((f32[64,1,128]{2,1,0:T(1,128)}), f32[64,1,128]{2,1,0:T(1,128)}, u32[]{:S(2)}, u32[]{:S(2)}) %all-to-all-start.2) | async-done | bytes 32800 | tf_op jit(solution)/shard_map/cond/branch_2_fun/all_to_all | solution.py:233
  178.1 0.0 collective-permute-done.23
  178.1 0.0 collective-permute-done.20
  178.1 0.1 pad_add_fusion.spot_ref
  178.2 5.5 %finish.1 = (bf16[128,5120]{1,0:T(8,128)(2,1)}, bf16[1536,128]{1,0:T(8,128)(2,1)}) custom-call(s32[2]{0:T(128)S(1)} %pad_add_fusion.spot_ref, bf16[128,5120]{1,0:T(8,128)(2,1)} %bitcast.56, bf16[128,5120]{1,0:T(8,128)(2,1)} %get-tuple-element.69.partner_ref, bf16[128,2560]{1,0:T(8,128)(2,1)} %get-tuple-element.70.here_ref, ...), custom_call_target="tpu_custom_call" | custom-call | flops 5242880 | bytes 8126464 | tf_op jit(solution)/shard_map/finish/pallas_call | solution.py:156
  (6 shorter events, 0.0 us)
Async XLA Ops:
  7.9 9.7 %copy-start.2 = (bf16[1,128,5120]{2,1,0:T(8,128)(2,1)S(1)}, bf16[1,128,5120]{2,1,0:T(8,128)(2,1)}, u32[]{:S(2)}) copy-start(bf16[1,128,5120]{2,1,0:T(8,128)(2,1)} %get-tuple-element.45) | copy-start | bytes 3932164 | tf_op jit(solution)/shard_map/cond
  7.9 117.9 %all-gather.8.cloned.1.call-start = ((), (), s32[]{:S(2)}) async-start(), calls=%async_computation.5 | async-start | bytes 8355840 | tf_op jit(solution)/shard_map/cond/branch_2_fun/all_gather | solution.py:217
  9.1 7.5 %collective-permute-start.17 = (bf16[48,2560]{1,0:T(8,128)(2,1)S(1)}, bf16[48,2560]{1,0:T(8,128)(2,1)S(1)}, u32[]{:S(2)}, u32[]{:S(2)}) collective-permute-start(bf16[48,2560]{1,0:T(8,128)(2,1)S(1)} %get-tuple-element.108), channel_id=1, source_target_pairs={{0,1},{1,0},{2,3},{3,2},{4,5},{5,4},{6,7},{7,6},{8,9},{9,8},{10,11... | collective-permute-start | bytes 737288 | tf_op jit(solution)/shard_map/cond/branch_2_fun/ppermute | solution.py:204
  17.5 11.3 %copy-start.5 = (bf16[1,1536,128]{2,1,0:T(8,128)(2,1)S(1)}, bf16[1,1536,128]{2,1,0:T(8,128)(2,1)}, u32[]{:S(2)}) copy-start(bf16[1,1536,128]{2,1,0:T(8,128)(2,1)} %get-tuple-element.94) | copy-start | bytes 1179652 | tf_op jit(solution)/shard_map/cond
  17.6 33.8 %collective-permute-start.18 = (bf16[128,5120]{1,0:T(8,128)(2,1)S(1)}, bf16[128,5120]{1,0:T(8,128)(2,1)}, u32[]{:S(2)}, u32[]{:S(2)}) collective-permute-start(bf16[128,5120]{1,0:T(8,128)(2,1)S(1)} %bitcast.59), channel_id=1, source_target_pairs={{0,128},{128,0},{1,129},{129,1},{2,130},{130,2},{3,131},{131,3},{4... | collective-permute-start | bytes 3932168 | tf_op jit(solution)/shard_map/cond/branch_2_fun/ppermute | solution.py:207
  25.7 24.4 %collective-permute-start.19 = (bf16[128,2560]{1,0:T(8,128)(2,1)}, bf16[128,2560]{1,0:T(8,128)(2,1)}, u32[]{:S(2)}, u32[]{:S(2)}) collective-permute-start(bf16[128,2560]{1,0:T(8,128)(2,1)} %get-tuple-element.106), channel_id=1, source_target_pairs={{0,1},{1,0},{2,3},{3,2},{4,5},{5,4},{6,7},{7,6},{8,9},{9,8},{10,11... | collective-permute-start | bytes 1966088 | tf_op jit(solution)/shard_map/cond/branch_2_fun/ppermute | solution.py:204
  29.0 21.1 %copy-start.8 = (bf16[128,2560]{1,0:T(8,128)(2,1)S(1)}, bf16[128,2560]{1,0:T(8,128)(2,1)}, u32[]{:S(2)}) copy-start(bf16[128,2560]{1,0:T(8,128)(2,1)} %get-tuple-element.105) | copy-start | bytes 1966084 | tf_op jit(solution)/shard_map/cond
  29.0 21.0 %collective-permute-start.16 = (bf16[1536,128]{0,1:T(8,128)(2,1)S(1)}, bf16[1536,128]{0,1:T(8,128)(2,1)S(1)}, u32[]{:S(2)}, u32[]{:S(2)}) collective-permute-start(bf16[1536,128]{0,1:T(8,128)(2,1)S(1)} %bitcast.64), channel_id=1, source_target_pairs={{0,1},{1,0},{2,3},{3,2},{4,5},{5,4},{6,7},{7,6},{8,9},{9,8},{10,11... | collective-permute-start | bytes 1179656 | tf_op jit(solution)/shard_map/cond/branch_2_fun/ppermute | solution.py:204
  131.2 46.9 %collective-permute-start.21 = (bf16[128,2560]{1,0:T(8,128)(2,1)}, bf16[128,2560]{1,0:T(8,128)(2,1)}, u32[]{:S(2)}, u32[]{:S(2)}) collective-permute-start(bf16[128,2560]{1,0:T(8,128)(2,1)} %get-tuple-element.129), channel_id=1, source_target_pairs={{0,128},{128,0},{1,129},{129,1},{2,130},{130,2},{3,131},{131,3},{4... | collective-permute-start | bytes 1966088 | tf_op jit(solution)/shard_map/cond/branch_2_fun/ppermute | solution.py:207
  135.8 42.3 %collective-permute-start.22 = (bf16[128,2560]{1,0:T(8,128)(2,1)S(1)}, bf16[128,2560]{1,0:T(8,128)(2,1)}, u32[]{:S(2)}, u32[]{:S(2)}) collective-permute-start(bf16[128,2560]{1,0:T(8,128)(2,1)S(1)} %get-tuple-element.53), channel_id=1, source_target_pairs={{0,129},{1,128},{128,1},{129,0},{2,131},{3,130},{130,3},{131,2},{4... | collective-permute-start | bytes 1966088 | tf_op jit(solution)/shard_map/cond/branch_2_fun/ppermute | solution.py:210
  138.9 39.2 %collective-permute-start.20 = (bf16[128,2560]{1,0:T(8,128)(2,1)S(1)}, bf16[128,2560]{1,0:T(8,128)(2,1)}, u32[]{:S(2)}, u32[]{:S(2)}) collective-permute-start(bf16[128,2560]{1,0:T(8,128)(2,1)S(1)} %get-tuple-element.53), channel_id=1, source_target_pairs={{0,1},{1,0},{2,3},{3,2},{4,5},{5,4},{6,7},{7,6},{8,9},{9,8},{10,11... | collective-permute-start | bytes 1966088 | tf_op jit(solution)/shard_map/cond/branch_2_fun/ppermute | solution.py:204
  145.7 32.4 %collective-permute-start.23 = (bf16[1536,128]{1,0:T(8,128)(2,1)S(1)}, bf16[1536,128]{1,0:T(8,128)(2,1)}, u32[]{:S(2)}, u32[]{:S(2)}) collective-permute-start(bf16[1536,128]{1,0:T(8,128)(2,1)S(1)} %get-tuple-element.49), channel_id=1, source_target_pairs={{0,1},{1,0},{2,3},{3,2},{4,5},{5,4},{6,7},{7,6},{8,9},{9,8},{10,11... | collective-permute-start | bytes 1179656 | tf_op jit(solution)/shard_map/cond/branch_2_fun/ppermute | solution.py:204
  148.8 29.3 %all-to-all-start.2 = ((f32[64,1,128]{2,1,0:T(1,128)}), f32[64,1,128]{2,1,0:T(1,128)}, u32[]{:S(2)}, u32[]{:S(2)}) async-start(f32[64,1,128]{2,1,0:T(1,128)} %bitcast.32), calls=%async_computation.2 | async-start | bytes 65536 | tf_op jit(solution)/shard_map/cond/branch_2_fun/all_to_all | solution.py:233
Sparse Core Ops, SparseCore 0:
  17.7 108.0 all-gather.7

commit v5 on v4

--- a/solution.py
+++ b/solution.py
@@ -104,9 +104,9 @@
     )(tokens, weight)
 
 
-def finish_kernel(
-    multiplier, spot_ref, weight_ref, partner_ref, here_ref, there_ref,
-    partner_here_ref, partner_there_ref, part_ref, from_pair_ref, squares_ref, new_ref, heads_ref,
+def average_kernel(
+    multiplier, spot_ref, weight_ref, partner_ref, here_ref, there_ref, partner_here_ref,
+    partner_there_ref, squares_ref, new_ref,
 ):
     entries = jnp.float32(4096 * 5120)
     own = spot_ref[1]
@@ -124,7 +124,7 @@
     def average(grad_ref, partner_grad_ref):
         mine = stepped(weight_ref, scale(own), grad_ref)
         theirs = stepped(partner_ref, scale(1 - own), partner_grad_ref)
-        new_ref[...] = (mine + theirs) * jnp.bfloat16(0.5)
+        new_ref[0] = (mine + theirs) * jnp.bfloat16(0.5)
 
     @pl.when(pl.program_id(0) == 0)
     def _():
@@ -134,54 +134,33 @@
     def _():
         average(there_ref, partner_there_ref)
 
-    heads_ref[...] = (
-        multiplier * (part_ref[...] + from_pair_ref[...].astype(jnp.float32))
-    ).astype(heads_ref.dtype)
-
-
-def finish(multiplier, spot, squares, weight, partner, grads, partner_grads, part, from_pair, blocks=1):
+
+def averaged(multiplier, spot, squares, weight, partner, grads, partner_grads):
     rows, width = weight.shape
     half = width // 2
-    cols = half // blocks
-    count = part.shape[0]
-    piece = count // (2 * blocks)
-
-    def whole(h, i, spot_ref):
-        return (0, jnp.where(h == 0, spot_ref[0], 1 - spot_ref[0]) * blocks + i)
-
-    first = lambda h, i, *_: (0, jnp.where(h == 0, i, blocks - 1))
-    second = lambda h, i, *_: (0, jnp.where(h == 0, 0, i))
-    down = lambda h, i, *_: (h * blocks + i, 0)
-    wide = pl.BlockSpec((rows, cols), whole)
+
+    def side(h, spot_ref):
+        return jnp.where(h == 0, spot_ref[0], 1 - spot_ref[0])
+
+    wide = pl.BlockSpec((rows, half), lambda h, spot_ref: (0, side(h, spot_ref)))
+    whole = pl.BlockSpec((rows, half), lambda h, spot_ref: (0, 0))
     return pl.pallas_call(
-        partial(finish_kernel, multiplier),
+        partial(average_kernel, multiplier),
         grid_spec=pltpu.PrefetchScalarGridSpec(
             num_scalar_prefetch=1,
-            grid=(2, blocks),
-            in_specs=[
-                wide,
-                wide,
-                pl.BlockSpec((rows, cols), first),
-                pl.BlockSpec((rows, cols), second),
-                pl.BlockSpec((rows, cols), first),
-                pl.BlockSpec((rows, cols), second),
-                pl.BlockSpec((piece, rows), down),
-                pl.BlockSpec((piece, rows), down),
-                pl.BlockSpec((SUMMED, 128), lambda h, i, *_: (0, 0)),
-            ],
-            out_specs=[wide, pl.BlockSpec((piece, rows), down)],
-        ),
-        out_shape=[
-            jax.ShapeDtypeStruct((rows, width), jnp.bfloat16),
-            jax.ShapeDtypeStruct((count, rows), jnp.bfloat16),
-        ],
+            grid=(2,),
+            in_specs=[wide, wide]
+            + [whole] * 4
+            + [pl.BlockSpec((SUMMED, 128), lambda h, spot_ref: (0, 0))],
+            out_specs=pl.BlockSpec((1, rows, half), lambda h, spot_ref: (0, 0, side(h, spot_ref))),
+        ),
+        out_shape=jax.ShapeDtypeStruct((1, rows, width), jnp.bfloat16),
         compiler_params=pltpu.CompilerParams(vmem_limit_bytes=VMEM_BYTES),
         cost_estimate=pl.CostEstimate(
-            flops=8 * rows * width, bytes_accessed=10 * rows * width + 8 * count * rows,
-            transcendentals=0,
-        ),
-        name="finish",
-    )(spot, weight, partner, *grads, *partner_grads, part, from_pair, squares)
+            flops=8 * rows * width, bytes_accessed=10 * rows * width, transcendentals=0
+        ),
+        name="averaged",
+    )(spot, weight, partner, *grads, *partner_grads, squares)
 
 
 def one_step(level, head_outputs, out_weight, cotangent):
@@ -220,42 +199,37 @@
     weight_pair = jnp.concatenate([mine(weight), swap(other(weight))], 0)
     partner_weight = to_partner(weight)
 
-    gathered, partner_weight, weight_pair = lax.optimization_barrier(
-        (gathered, partner_weight, weight_pair)
-    )
+    gathered, partner_weight, weight_pair, heads_t = lax.optimization_barrier(
+        (gathered, partner_weight, weight_pair, heads_t)
+    )
+    part_here, part_there = head_parts(gathered, weight_pair)
+    from_pair = swap(part_there)
+    heads_t, part_there = lax.optimization_barrier((heads_t, part_there))
     here, there, squares = gradient(heads_t, gathered)
     partner_there = across(there)
     there = swap(there)
     partner_here = to_partner(here)
-    part_here, part_there = head_parts(gathered, weight_pair)
-    from_pair = swap(part_there)
-    squares, part_there = lax.optimization_barrier((squares, part_there))
     squares = lax.all_to_all(squares, (partner_axis, *Z, "x"), 0, 0, tiled=True)
 
-    return (
-        own, squares, partner_weight, (here, there), (partner_here, partner_there), part_here,
-        from_pair,
-    )
-
-
-def per_device(step, head_outputs, out_weight, cotangent):
-    branches = [partial(one_step, level) for level in range(len(PARTNER_AXES))]
-    own, squares, partner_weight, grads, partner_grads, part_here, from_pair = lax.switch(
-        step[0] % len(PARTNER_AXES), branches, head_outputs, out_weight, cotangent
-    )
-    weight = out_weight[0]
-    new_weight, head_grads = finish(
-        float(weight.shape[0] * 32) ** (-0.5),
-        jnp.stack([lax.axis_index("x"), own]).astype(jnp.int32),
+    multiplier = float(rows * 32) ** (-0.5)
+    new_weight = averaged(
+        multiplier,
+        jnp.stack([x, own]).astype(jnp.int32),
         squares,
         weight,
         partner_weight,
-        grads,
-        partner_grads,
-        part_here,
-        from_pair,
-    )
-    return (new_weight[None], head_grads[None])
+        (here, there),
+        (partner_here, partner_there),
+    )
+    head_grads = (multiplier * (part_here + from_pair.astype(jnp.float32))).astype(jnp.bfloat16)
+    return new_weight, head_grads[None]
+
+
+def per_device(step, head_outputs, out_weight, cotangent):
+    branches = [partial(one_step, level) for level in range(len(PARTNER_AXES))]
+    return lax.switch(
+        step[0] % len(PARTNER_AXES), branches, head_outputs, out_weight, cotangent
+    )
 
 
 def solution(mesh):

time: 192 us -> 190 us (0.990)
  waiting for transfers between devices: 114 us -> 108 us
  other arithmetic: 2.17 us -> 4.27 us
    all_to_all x1, waiting for transfers between devices: 17.1 us -> 12.3 us  [one_step(): squares = lax.all_to_all(squares, (partner_axis, *Z, 'x'), 0, 0, tiled=True)]
    broadcast_in_dim x0 -> x1, other arithmetic: none -> 2.08 us  [one_step(): return (new_weight, head_grads[None])]
  transfers between devices with their start and end apart: 10 -> 10, of which waited for: 4 -> 4; matrix products, arithmetic and copies ran while one was open for 1% -> 3% of each run, Pallas kernels for 2% -> 3%
where the time goes in v5:
time: 190 us; the launch traced here: 187 us
  waiting for transfers between devices  108 us (57%)
  starting transfers between devices  41.2 us (22%)
  Pallas kernels  15.3 us (8%)
  between operations  14.7 us (8%)
  other arithmetic  4.27 us (2%)
  local copies, waits for them, and re-layouts  3.81 us (2%)
    all_gather x1, waiting for transfers between devices, one_step(): gathered = lax.all_gather(pair_tokens, Z, axis=0, tiled=True)  73.1 us
    ppermute x5, waiting for transfers between devices, swap(): return lax.ppermute(block, 'x', PAIR)  22.3 us
    ppermute x5, starting transfers between devices, swap(): return lax.ppermute(block, 'x', PAIR)  14.6 us
    all_to_all x1, waiting for transfers between devices, one_step(): squares = lax.all_to_all(squares, (partner_axis, *Z, 'x'), 0, 0, tiled=True)  12.3 us
    all_to_all x1, starting transfers between devices, one_step(): squares = lax.all_to_all(squares, (partner_axis, *Z, 'x'), 0, 0, tiled=True)  11.9 us
    ppermute x2, starting transfers between devices, to_partner(): return lax.ppermute(block, partner_axis, PAIR)  11.6 us
    pallas_call x1, Pallas kernels, gradient(): pl.pallas_call(gradient_kernel, grid=(blocks,), in_specs=[pl.BlockSpec((p...  5.54 us
    pallas_call x1, Pallas kernels, head_parts(): pl.pallas_call(head_parts_kernel, grid=(blocks,), in_specs=[pl.BlockSpec(...  5.25 us
  transfers between devices with their start and end apart: 10, of which 4 were waited for; matrix products, arithmetic and copies ran while one was open for 3% of the time, Pallas kernels for 3%

profile of v5, /device:TPU:1, one launch (start us, length us, event | category | flops | bytes accessed | tf_op | source)
XLA Modules:
  0.0 187.4 jit_solution(15176952598533127284)
XLA Ops:
  7.8 172.7 %conditional.1 = (bf16[1,128,5120]{2,1,0:T(8,128)(2,1)}, bf16[1,1536,128]{2,1,0:T(8,128)(2,1)}) conditional(s32[]{:T(128)} %clamp.3, (bf16[1,128,5120]{2,1,0:T(8,128)(2,1)}, bf16[1,48,5120]{2,1,0:T(8,128)(2,1)}, bf16[1,1536,128]{2,1,0:T(8,128)(2,1)}) %tuple.25, (bf16[1,128,5120]{2,1,0:T(8,128)(2,1)}, bf16[1,48,5120]{2,1,0:T(8,128)(2,1)}, ...), branch_computations={%region_0.1_spmd, %region_1.2_spmd, %region_2.3_spmd} | conditional | flops 4038967296 | bytes 90374832 | solution.py:230
  8.0 0.0 all-gather.8.cloned.1.call-start
  8.1 1.1 dynamic-slice_bitcast_fusion.11
  9.2 3.9 %collective-permute-start.16 = (bf16[48,2560]{1,0:T(8,128)(2,1)S(1)}, bf16[48,2560]{1,0:T(8,128)(2,1)S(1)}, u32[]{:S(2)}, u32[]{:S(2)}) collective-permute-start(bf16[48,2560]{1,0:T(8,128)(2,1)S(1)} %get-tuple-element.90), channel_id=1, source_target_pairs={{0,1},{1,0},{2,3},{3,2},{4,5},{5,4},{6,7},{7,6},{8,9},{9,8},{10,11... | collective-permute-start | bytes 737288 | tf_op jit(solution)/shard_map/cond/branch_2_fun/ppermute | solution.py:183
  13.2 3.6 %collective-permute-done.16 = bf16[48,2560]{1,0:T(8,128)(2,1)S(1)} collective-permute-done((bf16[48,2560]{1,0:T(8,128)(2,1)S(1)}, bf16[48,2560]{1,0:T(8,128)(2,1)S(1)}, u32[]{:S(2)}, u32[]{:S(2)}) %collective-permute-start.16) | collective-permute-done | bytes 245792 | tf_op jit(solution)/shard_map/cond/branch_2_fun/ppermute | solution.py:183
  16.7 0.9 maximum_select_fusion.2
  17.6 0.0 all-gather.8.cloned.1.call-update
  17.6 0.0 copy-start.5
  17.6 7.0 %collective-permute-start.17 = (bf16[128,5120]{1,0:T(8,128)(2,1)}, bf16[128,5120]{1,0:T(8,128)(2,1)S(1)}, u32[]{:S(2)}, u32[]{:S(2)}) collective-permute-start(bf16[128,5120]{1,0:T(8,128)(2,1)} %bitcast.30.weight_ref), channel_id=1, source_target_pairs={{0,128},{128,0},{1,129},{129,1},{2,130},{130,2},{3,131},{131,3},{4... | collective-permute-start | bytes 3932168 | tf_op jit(solution)/shard_map/cond/branch_2_fun/ppermute | solution.py:186
  24.6 2.5 %dynamic-slice_bitcast_fusion.9 = (bf16[128,2560]{1,0:T(8,128)(2,1)}, bf16[128,2560]{1,0:T(8,128)(2,1)}) fusion(bf16[1,128,5120]{2,1,0:T(8,128)(2,1)} %get-tuple-element.44, s32[]{:T(128)S(6)} %select_n.47, s32[]{:T(128)S(6)} %select_n.48), kind=kLoop, calls=%fused_computation.24 | loop fusion | bytes 2621448 | tf_op jit(solution)/shard_map/cond/branch_2_fun/dynamic_slice | solution.py:177
  27.1 3.1 %collective-permute-start.18 = (bf16[128,2560]{1,0:T(8,128)(2,1)}, bf16[128,2560]{1,0:T(8,128)(2,1)}, u32[]{:S(2)}, u32[]{:S(2)}) collective-permute-start(bf16[128,2560]{1,0:T(8,128)(2,1)} %get-tuple-element.88), channel_id=1, source_target_pairs={{0,1},{1,0},{2,3},{3,2},{4,5},{5,4},{6,7},{7,6},{8,9},{9,8},{10,11... | collective-permute-start | bytes 1966088 | tf_op jit(solution)/shard_map/cond/branch_2_fun/ppermute | solution.py:183
  30.3 0.2 copy.20
  30.4 0.0 copy-start.8
  30.5 2.3 %collective-permute-start.19 = (bf16[1536,128]{0,1:T(8,128)(2,1)S(1)}, bf16[1536,128]{0,1:T(8,128)(2,1)S(1)}, u32[]{:S(2)}, u32[]{:S(2)}) collective-permute-start(bf16[1536,128]{0,1:T(8,128)(2,1)S(1)} %bitcast.68), channel_id=1, source_target_pairs={{0,1},{1,0},{2,3},{3,2},{4,5},{5,4},{6,7},{7,6},{8,9},{9,8},{10,11... | collective-permute-start | bytes 1179656 | tf_op jit(solution)/shard_map/cond/branch_2_fun/ppermute | solution.py:183
  32.8 18.7 %collective-permute-done.19 = bf16[1536,128]{0,1:T(8,128)(2,1)S(1)} collective-permute-done((bf16[1536,128]{0,1:T(8,128)(2,1)S(1)}, bf16[1536,128]{0,1:T(8,128)(2,1)S(1)}, u32[]{:S(2)}, u32[]{:S(2)}) %collective-permute-start.19) | collective-permute-done | bytes 393248 | tf_op jit(solution)/shard_map/cond/branch_2_fun/ppermute | solution.py:183
  51.5 0.1 maximum_bitcast_fusion.2.heads_ref
  51.5 0.0 collective-permute-done.18
  51.5 1.2 pad_maximum_fusion.2.weight_ref
  52.7 0.0 collective-permute-done.17.partner_ref
  52.7 73.1 %all-gather.8.cloned.1.call-done.tokens_ref = bf16[1536,2560]{1,0:T(8,128)(2,1)} async-done(((bf16[96,2560]{1,0:T(8,128)(2,1)}), bf16[1536,2560]{1,0:T(8,128)(2,1)}) %all-gather.8.cloned.1.call-update) | async-done | bytes 7864336 | tf_op jit(solution)/shard_map/cond/branch_2_fun/all_gather | solution.py:196
  125.8 5.3 %head_parts.5 = (f32[1536,128]{1,0:T(8,128)S(1)}, bf16[1536,128]{1,0:T(8,128)(2,1)}) custom-call(bf16[1536,2560]{1,0:T(8,128)(2,1)} %all-gather.8.cloned.1.call-done.tokens_ref, bf16[256,2560]{1,0:T(8,128)(2,1)S(1)} %pad_maximum_fusion.2.weight_ref), custom_call_target="tpu_custom_call" | custom-call | flops 2013265920 | bytes 10354688 | tf_op jit(solution)/shard_map/cond/branch_2_fun/head_parts/pallas_call | solution.py:85
  131.1 3.1 %collective-permute-start.23 = (bf16[1536,128]{1,0:T(8,128)(2,1)}, bf16[1536,128]{1,0:T(8,128)(2,1)}, u32[]{:S(2)}, u32[]{:S(2)}) collective-permute-start(bf16[1536,128]{1,0:T(8,128)(2,1)} %get-tuple-element.51), channel_id=1, source_target_pairs={{0,1},{1,0},{2,3},{3,2},{4,5},{5,4},{6,7},{7,6},{8,9},{9,8},{10,11... | collective-permute-start | bytes 1179656 | tf_op jit(solution)/shard_map/cond/branch_2_fun/ppermute | solution.py:183
  134.1 5.5 %gradient.5 = (bf16[128,2560]{1,0:T(8,128)(2,1)S(1)}, bf16[128,2560]{1,0:T(8,128)(2,1)}, f32[64,128]{1,0:T(8,128)}) custom-call(bf16[256,1536]{1,0:T(8,128)(2,1)S(1)} %maximum_bitcast_fusion.2.heads_ref, bf16[1536,2560]{1,0:T(8,128)(2,1)} %all-gather.8.cloned.1.call-done.tokens_ref), custom_call_target="tpu_custom_call" | custom-call | flops 2013265920 | bytes 9961472 | tf_op jit(solution)/shard_map/cond/branch_2_fun/gradient/pallas_call | solution.py:43
  139.7 2.2 %collective-permute-start.20 = (bf16[128,2560]{1,0:T(8,128)(2,1)}, bf16[128,2560]{1,0:T(8,128)(2,1)S(1)}, u32[]{:S(2)}, u32[]{:S(2)}) collective-permute-start(bf16[128,2560]{1,0:T(8,128)(2,1)} %get-tuple-element.54), channel_id=1, source_target_pairs={{0,1},{1,0},{2,3},{3,2},{4,5},{5,4},{6,7},{7,6},{8,9},{9,8},{10,11... | collective-permute-start | bytes 1966088 | tf_op jit(solution)/shard_map/cond/branch_2_fun/ppermute | solution.py:183
  141.9 4.6 %collective-permute-start.21 = (bf16[128,2560]{1,0:T(8,128)(2,1)S(1)}, bf16[128,2560]{1,0:T(8,128)(2,1)S(1)}, u32[]{:S(2)}, u32[]{:S(2)}) collective-permute-start(bf16[128,2560]{1,0:T(8,128)(2,1)S(1)} %get-tuple-element.53.here_ref), channel_id=1, source_target_pairs={{0,128},{128,0},{1,129},{129,1},{2,130},{130,2},{3,131},{131,3},{4... | collective-permute-start | bytes 1966088 | tf_op jit(solution)/shard_map/cond/branch_2_fun/ppermute | solution.py:186
  146.5 3.1 %collective-permute-start.22 = (bf16[128,2560]{1,0:T(8,128)(2,1)}, bf16[128,2560]{1,0:T(8,128)(2,1)}, u32[]{:S(2)}, u32[]{:S(2)}) collective-permute-start(bf16[128,2560]{1,0:T(8,128)(2,1)} %get-tuple-element.54), channel_id=1, source_target_pairs={{0,129},{1,128},{128,1},{129,0},{2,131},{3,130},{130,3},{131,2},{4... | collective-permute-start | bytes 1966088 | tf_op jit(solution)/shard_map/cond/branch_2_fun/ppermute | solution.py:189
  149.6 0.1 pad_add_fusion.2.spot_ref
  149.7 11.9 %all-to-all-start.2 = ((f32[64,1,128]{2,1,0:T(1,128)}), f32[64,1,128]{2,1,0:T(1,128)S(1)}, u32[]{:S(2)}, u32[]{:S(2)}) async-start(f32[64,1,128]{2,1,0:T(1,128)} %bitcast.38), calls=%async_computation.2 | async-start | bytes 65536 | tf_op jit(solution)/shard_map/cond/branch_2_fun/all_to_all | solution.py:212
  161.6 2.1 %fusion.2 = bf16[1,1536,128]{2,1,0:T(8,128)(2,1)} fusion(f32[1536,128]{1,0:T(8,128)} %copy-done.2, bf16[1536,128]{1,0:T(8,128)(2,1)} %collective-permute-done.23), kind=kLoop, calls=%fused_computation.26 | loop fusion | flops 786432 | bytes 1572864 | tf_op jit(solution)/shard_map/cond/branch_2_fun/broadcast_in_dim | solution.py:225
  163.7 12.3 %all-to-all-done.2 = f32[64,1,128]{2,1,0:T(1,128)S(1)} async-done(((f32[64,1,128]{2,1,0:T(1,128)}), f32[64,1,128]{2,1,0:T(1,128)S(1)}, u32[]{:S(2)}, u32[]{:S(2)}) %all-to-all-start.2) | async-done | bytes 32800 | tf_op jit(solution)/shard_map/cond/branch_2_fun/all_to_all | solution.py:212
  176.0 0.0 collective-permute-done.20.there_ref
  176.0 4.5 %averaged.5 = bf16[1,128,5120]{2,1,0:T(8,128)(2,1)} custom-call(s32[2]{0:T(128)S(1)} %pad_add_fusion.2.spot_ref, bf16[128,5120]{1,0:T(8,128)(2,1)} %bitcast.30.weight_ref, bf16[128,5120]{1,0:T(8,128)(2,1)S(1)} %collective-permute-done.17.partner_ref, bf16[128,2560]{1,0:T(8,128)(2,1)S(1)} %get-tuple-element.53.here_ref, ...), custom_call_target="tpu_custom_call" | custom-call | flops 5242880 | bytes 6553600 | tf_op jit(solution)/shard_map/cond/branch_2_fun/averaged/pallas_call | solution.py:147
  (7 shorter events, 0.0 us)
Async XLA Ops:
  8.0 117.8 %all-gather.8.cloned.1.call-start = ((), (), s32[]{:S(2)}) async-start(), calls=%async_computation.5 | async-start | bytes 8355840 | tf_op jit(solution)/shard_map/cond/branch_2_fun/all_gather | solution.py:196
  9.2 7.5 %collective-permute-start.16 = (bf16[48,2560]{1,0:T(8,128)(2,1)S(1)}, bf16[48,2560]{1,0:T(8,128)(2,1)S(1)}, u32[]{:S(2)}, u32[]{:S(2)}) collective-permute-start(bf16[48,2560]{1,0:T(8,128)(2,1)S(1)} %get-tuple-element.90), channel_id=1, source_target_pairs={{0,1},{1,0},{2,3},{3,2},{4,5},{5,4},{6,7},{7,6},{8,9},{9,8},{10,11... | collective-permute-start | bytes 737288 | tf_op jit(solution)/shard_map/cond/branch_2_fun/ppermute | solution.py:183
  17.6 12.6 %copy-start.5 = (bf16[1,1536,128]{2,1,0:T(8,128)(2,1)S(1)}, bf16[1,1536,128]{2,1,0:T(8,128)(2,1)}, u32[]{:S(2)}) copy-start(bf16[1,1536,128]{2,1,0:T(8,128)(2,1)} %get-tuple-element.78) | copy-start | bytes 1179652 | tf_op jit(solution)/shard_map/cond
  17.6 35.1 %collective-permute-start.17 = (bf16[128,5120]{1,0:T(8,128)(2,1)}, bf16[128,5120]{1,0:T(8,128)(2,1)S(1)}, u32[]{:S(2)}, u32[]{:S(2)}) collective-permute-start(bf16[128,5120]{1,0:T(8,128)(2,1)} %bitcast.30.weight_ref), channel_id=1, source_target_pairs={{0,128},{128,0},{1,129},{129,1},{2,130},{130,2},{3,131},{131,3},{4... | collective-permute-start | bytes 3932168 | tf_op jit(solution)/shard_map/cond/branch_2_fun/ppermute | solution.py:186
  27.1 24.4 %collective-permute-start.18 = (bf16[128,2560]{1,0:T(8,128)(2,1)}, bf16[128,2560]{1,0:T(8,128)(2,1)}, u32[]{:S(2)}, u32[]{:S(2)}) collective-permute-start(bf16[128,2560]{1,0:T(8,128)(2,1)} %get-tuple-element.88), channel_id=1, source_target_pairs={{0,1},{1,0},{2,3},{3,2},{4,5},{5,4},{6,7},{7,6},{8,9},{9,8},{10,11... | collective-permute-start | bytes 1966088 | tf_op jit(solution)/shard_map/cond/branch_2_fun/ppermute | solution.py:183
  30.4 21.1 %copy-start.8 = (bf16[128,2560]{1,0:T(8,128)(2,1)S(1)}, bf16[128,2560]{1,0:T(8,128)(2,1)}, u32[]{:S(2)}) copy-start(bf16[128,2560]{1,0:T(8,128)(2,1)} %get-tuple-element.87) | copy-start | bytes 1966084 | tf_op jit(solution)/shard_map/cond
  30.5 21.0 %collective-permute-start.19 = (bf16[1536,128]{0,1:T(8,128)(2,1)S(1)}, bf16[1536,128]{0,1:T(8,128)(2,1)S(1)}, u32[]{:S(2)}, u32[]{:S(2)}) collective-permute-start(bf16[1536,128]{0,1:T(8,128)(2,1)S(1)} %bitcast.68), channel_id=1, source_target_pairs={{0,1},{1,0},{2,3},{3,2},{4,5},{5,4},{6,7},{7,6},{8,9},{9,8},{10,11... | collective-permute-start | bytes 1179656 | tf_op jit(solution)/shard_map/cond/branch_2_fun/ppermute | solution.py:183
  131.1 8.6 %copy-start.2 = (f32[1536,128]{1,0:T(8,128)}, f32[1536,128]{1,0:T(8,128)S(1)}, u32[]{:S(2)}) copy-start(f32[1536,128]{1,0:T(8,128)S(1)} %get-tuple-element.56) | copy-start | bytes 2359300 | tf_op jit(solution)/shard_map/cond
  131.1 30.5 %collective-permute-start.23 = (bf16[1536,128]{1,0:T(8,128)(2,1)}, bf16[1536,128]{1,0:T(8,128)(2,1)}, u32[]{:S(2)}, u32[]{:S(2)}) collective-permute-start(bf16[1536,128]{1,0:T(8,128)(2,1)} %get-tuple-element.51), channel_id=1, source_target_pairs={{0,1},{1,0},{2,3},{3,2},{4,5},{5,4},{6,7},{7,6},{8,9},{9,8},{10,11... | collective-permute-start | bytes 1179656 | tf_op jit(solution)/shard_map/cond/branch_2_fun/ppermute | solution.py:183
  139.7 36.3 %collective-permute-start.20 = (bf16[128,2560]{1,0:T(8,128)(2,1)}, bf16[128,2560]{1,0:T(8,128)(2,1)S(1)}, u32[]{:S(2)}, u32[]{:S(2)}) collective-permute-start(bf16[128,2560]{1,0:T(8,128)(2,1)} %get-tuple-element.54), channel_id=1, source_target_pairs={{0,1},{1,0},{2,3},{3,2},{4,5},{5,4},{6,7},{7,6},{8,9},{9,8},{10,11... | collective-permute-start | bytes 1966088 | tf_op jit(solution)/shard_map/cond/branch_2_fun/ppermute | solution.py:183
  141.9 34.1 %collective-permute-start.21 = (bf16[128,2560]{1,0:T(8,128)(2,1)S(1)}, bf16[128,2560]{1,0:T(8,128)(2,1)S(1)}, u32[]{:S(2)}, u32[]{:S(2)}) collective-permute-start(bf16[128,2560]{1,0:T(8,128)(2,1)S(1)} %get-tuple-element.53.here_ref), channel_id=1, source_target_pairs={{0,128},{128,0},{1,129},{129,1},{2,130},{130,2},{3,131},{131,3},{4... | collective-permute-start | bytes 1966088 | tf_op jit(solution)/shard_map/cond/branch_2_fun/ppermute | solution.py:186
  146.5 29.5 %collective-permute-start.22 = (bf16[128,2560]{1,0:T(8,128)(2,1)}, bf16[128,2560]{1,0:T(8,128)(2,1)}, u32[]{:S(2)}, u32[]{:S(2)}) collective-permute-start(bf16[128,2560]{1,0:T(8,128)(2,1)} %get-tuple-element.54), channel_id=1, source_target_pairs={{0,129},{1,128},{128,1},{129,0},{2,131},{3,130},{130,3},{131,2},{4... | collective-permute-start | bytes 1966088 | tf_op jit(solution)/shard_map/cond/branch_2_fun/ppermute | solution.py:189
  149.7 26.4 %all-to-all-start.2 = ((f32[64,1,128]{2,1,0:T(1,128)}), f32[64,1,128]{2,1,0:T(1,128)S(1)}, u32[]{:S(2)}, u32[]{:S(2)}) async-start(f32[64,1,128]{2,1,0:T(1,128)} %bitcast.38), calls=%async_computation.2 | async-start | bytes 65536 | tf_op jit(solution)/shard_map/cond/branch_2_fun/all_to_all | solution.py:212
Sparse Core Ops, SparseCore 0:
  17.7 108.0 all-gather.7
